TPU v7x, 32 devices: a whole 2x2x4 slice. The times are simulated.
32 devices in a mesh: seq: 16 (over z, y, core), head: 2 (over x).
Axes of the slice: x: 2, y: 2, z: 4, core: 2. Of those that a mesh axis runs over, the one named last changes fastest.
Arguments:
- queries: bfloat16 [4096, 2048], P(('seq', 'head')), may hold values from -28 to 28
- key_states: bfloat16 [4096, 512], P(('seq', 'head')), may hold values from -20 to 20
- value_vector_rows: bfloat16 [4096, 512], P(('seq', 'head')), may hold values from -6 to 6
- grad_output: bfloat16 [4096, 2048], P(('seq', 'head')), may hold values from -6 to 6
- doc_ids: int32 [32], replicated, may hold values from 0 to 3, never falling along the last dimension, each value on 1 to 16 neighbouring positions
- block_home: int32 [32], replicated, may hold values from 0 to 31, as said below
Outputs:
- attended: bfloat16 [4096, 2048], P('seq', 'head')
- grad_query: bfloat16 [4096, 2048], P('seq', 'head')
- key_gradient: bfloat16 [4096, 512], P('seq', 'head')
- value_gradient: bfloat16 [4096, 512], P('seq', 'head')
Inputs may be any that keep to these rules, and one draw needn't show every extreme that they name: `block_home`: a permutation of the natural blocks; slots are numbered shard by shard, 2 slots to a seq shard; every block sits in its natural shard (block // 2) or one beside it, and across each boundary between neighbouring shards exactly one block moves each way.
All inputs are finite; a program needn't handle non-finite values.
Results may differ from a plain program's by a relative error of at most 0.025.
Values may be sent and summed in bfloat16 or wider, within the bound.
No kernel may reach another device: no remote copies, remote signals or barrier semaphores. Data moves between devices by JAX's collectives and lax.ppermute only.
A program may use at most 192 MiB of HBM per device.

v0:
```python
import math

import jax
import jax.numpy as jnp
from jax import lax
from jax.sharding import PartitionSpec as P

BLK = 128
WINDOW = 2048
HEAD_SIZE = 128


def with_halo(cells, sides, width):
    for axis, dim in sides:
        count = lax.axis_size(axis)
        ends = count - 1
        head = lax.slice_in_dim(cells, 0, width, axis=dim)
        tail = lax.slice_in_dim(cells, cells.shape[dim] - width, cells.shape[dim], axis=dim)
        cells = jnp.concatenate(
            [
                lax.ppermute(tail, axis, [(i, (i + 1) % count) for i in range(ends)]),
                cells,
                lax.ppermute(head, axis, [((i + 1) % count, i) for i in range(ends)]),
            ],
            axis=dim,
        )
    return cells


def passed_along(block, axis, distance):
    devices = range(lax.axis_size(axis))
    route = [(i - distance, i) for i in devices if i - distance in devices]
    return lax.ppermute(block, axis, route)


def per_device(queries, key_states, value_vector_rows, grad_output, doc_ids, block_home):
    seq_at = lax.axis_index("seq")
    arrived = (
        lax.all_to_all(queries, "head", split_axis=1, concat_axis=0, tiled=True),
        lax.all_to_all(key_states, "head", split_axis=1, concat_axis=0, tiled=True),
        lax.all_to_all(value_vector_rows, "head", split_axis=1, concat_axis=0, tiled=True),
        lax.all_to_all(grad_output, "head", split_axis=1, concat_axis=0, tiled=True),
    )
    tokens_dev = arrived[0].shape[0]
    block_count = tokens_dev // BLK
    widths_list = [member.shape[1] for member in arrived]
    packed = jnp.concatenate(list(arrived), axis=1)
    width_all = packed.shape[1]
    block_total = doc_ids.shape[0]
    listing = jnp.arange(block_total, dtype=jnp.int32)
    wanted = seq_at * block_count + jnp.arange(block_count, dtype=jnp.int32)
    owners = jnp.sum(jnp.where(block_home[None, :] == wanted[:, None], listing[None, :], 0), axis=1)
    beside_all = with_halo(packed, (("seq", 0),), tokens_dev)
    offsets = (owners - (seq_at - 1) * block_count) * BLK
    natural = jax.vmap(lambda first_row: lax.dynamic_slice_in_dim(beside_all, first_row, BLK, 0))(
        offsets
    ).reshape(tokens_dev, width_all)
    edge_one = widths_list[0]
    edge_two = edge_one + widths_list[1]
    edge_three = edge_two + widths_list[2]
    query_natural_order = natural[:, :edge_one]
    key_natural_order = natural[:, edge_one:edge_two]
    value_natural_order = natural[:, edge_two:edge_three]
    gradient_natural_order = natural[:, edge_three:]
    kv_heads = key_natural_order.shape[1] // HEAD_SIZE
    queries_per_group = query_natural_order.shape[1] // key_natural_order.shape[1]
    key_width = kv_heads * HEAD_SIZE
    reciprocal_root = 1.0 / math.sqrt(HEAD_SIZE)
    query_four = query_natural_order.reshape(tokens_dev, kv_heads, queries_per_group, HEAD_SIZE)
    grad_four = gradient_natural_order.reshape(tokens_dev, kv_heads, queries_per_group, HEAD_SIZE)
    key_value = jnp.concatenate([key_natural_order, value_natural_order], axis=1)
    reach = WINDOW // tokens_dev
    tails = [passed_along(key_value, "seq", back) for back in range(1, reach + 1)]
    stacked = jnp.stack([key_value] + tails)
    padded_doc = jnp.concatenate([jnp.full((reach * block_count,), -1, jnp.int32), doc_ids])
    distances = jnp.arange(reach + 1, dtype=jnp.int32)
    key_docs = jax.vmap(
        lambda back: jnp.repeat(
            lax.dynamic_slice_in_dim(
                padded_doc, (seq_at - back + reach) * block_count, block_count, 0
            ),
            BLK,
        )
    )(distances)
    query_doc = jnp.repeat(
        lax.dynamic_slice_in_dim(doc_ids, seq_at * block_count, block_count, 0), BLK
    )
    positions = jnp.arange(tokens_dev, dtype=jnp.int32)

    def visible_of(back, key_doc):
        distance = back * tokens_dev + positions[:, None] - positions[None, :]
        return (query_doc[:, None] == key_doc[None, :]) & (distance >= 0) & (distance < WINDOW)

    def split_block(block):
        local_keys = block[:, :key_width].reshape(tokens_dev, kv_heads, HEAD_SIZE)
        local_values = block[:, key_width:].reshape(tokens_dev, kv_heads, HEAD_SIZE)
        return (local_keys, local_values)

    visible_all = jax.vmap(visible_of)(distances, key_docs)

    def score_pass(carried, entry):
        block, visible = entry
        local_keys, local_values = split_block(block)
        kept = (
            jnp.einsum("tgqd,ugd->gqtu", query_four, local_keys, preferred_element_type=jnp.float32)
            * reciprocal_root
        )
        return (carried, kept)

    unused_one, scores_all = lax.scan(score_pass, 0, (stacked, visible_all))
    seen = visible_all[:, None, None, :, :]
    final_max = jnp.max(jnp.where(seen, scores_all, -1e30), axis=(0, 4))
    final_sum = jnp.sum(
        jnp.where(seen, jnp.exp(scores_all - final_max[None, ..., None]), 0.0), axis=(0, 4)
    )
    log_total = final_max + jnp.log(final_sum)

    def second_pass(carried, entry):
        block, visible, scores = entry
        local_keys, local_values = split_block(block)
        probability_lowered = jnp.where(
            visible, jnp.exp(scores - log_total[..., None]), 0.0
        ).astype(jnp.bfloat16)
        return (
            carried
            + jnp.einsum(
                "gqtu,ugd->tgqd",
                probability_lowered,
                local_values,
                preferred_element_type=jnp.float32,
            ),
            None,
        )

    out_start = jnp.zeros((tokens_dev, kv_heads, queries_per_group, HEAD_SIZE), jnp.float32)
    out_accum, unused_two = lax.scan(second_pass, out_start, (stacked, visible_all, scores_all))
    attended = out_accum.astype(jnp.bfloat16)
    delta = jnp.einsum("tgqd,tgqd->gqt", grad_four, attended, preferred_element_type=jnp.float32)

    def gradients(block, visible, scores):
        local_keys, local_values = split_block(block)
        prob = jnp.where(visible, jnp.exp(scores - log_total[..., None]), 0.0)
        probability_lowered = prob.astype(jnp.bfloat16)
        grad_prob = jnp.einsum(
            "tgqd,ugd->gqtu", grad_four, local_values, preferred_element_type=jnp.float32
        )
        score_gradient = (prob * (grad_prob - delta[..., None])).astype(jnp.bfloat16)
        query_term = jnp.einsum(
            "gqtu,ugd->tgqd", score_gradient, local_keys, preferred_element_type=jnp.float32
        )
        key_contribution = jnp.einsum(
            "nzev,enzx->vnx", score_gradient, query_four, preferred_element_type=jnp.float32
        ).reshape(tokens_dev, key_width)
        value_contribution = jnp.einsum(
            "nzev,enzx->vnx", probability_lowered, grad_four, preferred_element_type=jnp.float32
        ).reshape(tokens_dev, key_width)
        return (query_term, jnp.concatenate([key_contribution, value_contribution], axis=1))

    query_accum, dkv_total = gradients(stacked[0], visible_all[0], scores_all[0])
    for back in range(1, reach + 1):
        query_term, shard_term = gradients(stacked[back], visible_all[back], scores_all[back])
        query_accum = query_accum + query_term
        dkv_total = dkv_total + passed_along(shard_term.astype(jnp.bfloat16), "seq", -back).astype(
            shard_term.dtype
        )
    attended_out = attended.reshape(tokens_dev, kv_heads * queries_per_group * HEAD_SIZE)
    grad_query = (
        (query_accum * reciprocal_root)
        .astype(jnp.bfloat16)
        .reshape(tokens_dev, kv_heads * queries_per_group * HEAD_SIZE)
    )
    key_gradient = (dkv_total[:, :key_width] * reciprocal_root).astype(jnp.bfloat16)
    value_gradient = dkv_total[:, key_width:].astype(jnp.bfloat16)
    return (attended_out, grad_query, key_gradient, value_gradient)


def solution(mesh):
    return jax.shard_map(
        per_device,
        mesh=mesh,
        in_specs=(
            P(("seq", "head"), None),
            P(("seq", "head"), None),
            P(("seq", "head"), None),
            P(("seq", "head"), None),
            P(),
            P(),
        ),
        out_specs=(P("seq", "head"), P("seq", "head"), P("seq", "head"), P("seq", "head")),
        check_vma=False,
    )
```

profile of v0, /device:TPU:17, one launch (start us, length us, event | category | flops | bytes accessed | tf_op | source)
XLA Modules:
  0.0 419.7 jit_solution(13846004672382899513)
XLA Ops:
  2.3 3.4 all-to-all-start.1
  9.0 3.4 all-to-all-start.2
  15.7 3.5 all-to-all-start.3
  20.2 4.4 %all-to-all-done.3 = bf16[128,2,1024]{2,0,1:T(8,128)(2,1)S(1)} async-done(((bf16[128,2,1024]{2,0,1:T(8,128)(2,1)}), bf16[128,2,1024]{2,0,1:T(8,128)(2,1)S(1)}, u32[]{:S(2)}, u32[]{:S(2)}) %all-to-all-start.3) | async-done | bytes 524320 | tf_op jit(solution)/shard_map/all_to_all | solution.py:42
  24.6 3.5 all-to-all-start
  29.0 4.4 %all-to-all-done = bf16[128,2,1024]{2,0,1:T(8,128)(2,1)S(1)} async-done(((bf16[128,2,1024]{2,0,1:T(8,128)(2,1)}), bf16[128,2,1024]{2,0,1:T(8,128)(2,1)S(1)}, u32[]{:S(2)}, u32[]{:S(2)}) %all-to-all-start) | async-done | bytes 524320 | tf_op jit(solution)/shard_map/all_to_all | solution.py:39
  34.6 8.3 %collective-permute-start = (bf16[256,2560]{1,0:T(8,128)(2,1)}, bf16[256,2560]{1,0:T(8,128)(2,1)}, u32[]{:S(2)}, u32[]{:S(2)}) collective-permute-start(bf16[256,2560]{1,0:T(8,128)(2,1)} %pad_maximum_fusion.1), channel_id=1, source_target_pairs={{0,2},{2,4},{4,6},{6,8},{8,10},{10,12},{12,14},{14,16},{16,18},{18... | collective-permute-start | bytes 3932168 | tf_op jit(solution)/shard_map/ppermute | solution.py:21
  54.0 17.9 %collective-permute-done = bf16[256,2560]{1,0:T(8,128)(2,1)} collective-permute-done((bf16[256,2560]{1,0:T(8,128)(2,1)}, bf16[256,2560]{1,0:T(8,128)(2,1)}, u32[]{:S(2)}, u32[]{:S(2)}) %collective-permute-start) | collective-permute-done | bytes 1310752 | tf_op jit(solution)/shard_map/ppermute | solution.py:21
  73.4 3.7 pad_maximum_fusion
  77.1 4.3 %while.26 = (s32[]{:T(128)}, bf16[768,2560]{1,0:T(8,128)(2,1)}, s32[2,2]{1,0:T(2,128)S(1)}, bf16[2,128,2560]{2,1,0:T(8,128)(2,1)}) while((s32[]{:T(128)}, bf16[768,2560]{1,0:T(8,128)(2,1)}, s32[2,2]{1,0:T(2,128)S(1)}, bf16[2,128,2560]{2,1,0:T(8,128)(2,1)}) %tuple.91), condition=%wide.while_cond.clone, body=%wide.while_body.sunk.clone | while | flops 2 | bytes 1311309 | solution.py:55
  83.2 2.8 collective-permute-start.2
  88.0 2.7 collective-permute-start.4
  113.6 6.2 %collective-permute-done.7 = bf16[256,512]{0,1:T(8,128)(2,1)S(1)} collective-permute-done((bf16[256,512]{0,1:T(8,128)(2,1)}, bf16[256,512]{0,1:T(8,128)(2,1)S(1)}, u32[]{:S(2)}, u32[]{:S(2)}) %collective-permute-start.7) | collective-permute-done | bytes 262176 | tf_op jit(solution)/shard_map/ppermute | solution.py:33
  120.5 4.7 %collective-permute-done.8 = bf16[256,512]{0,1:T(8,128)(2,1)S(1)} collective-permute-done((bf16[256,512]{0,1:T(8,128)(2,1)}, bf16[256,512]{0,1:T(8,128)(2,1)S(1)}, u32[]{:S(2)}, u32[]{:S(2)}) %collective-permute-start.8) | collective-permute-done | bytes 262176 | tf_op jit(solution)/shard_map/ppermute | solution.py:33
  126.8 25.3 %while.25 = (s32[]{:T(128)}, f32[9,2,4,256,256]{3,4,2,1,0:T(8,128)}, bf16[9,256,512]{1,2,0:T(8,128)(2,1)}, bf16[256,2,4,128]{3,0,2,1:T(8,128)(2,1)S(1)}) while((s32[]{:T(128)}, f32[9,2,4,256,256]{3,4,2,1,0:T(8,128)}, bf16[9,256,512]{1,2,0:T(8,128)(2,1)}, bf16[256,2,4,128]{3,0,2,1:T(8,128)(2,1)S(1)}) %tuple.94), condition=%wide.region_2.3_spmd.clone, body=%wide.region_1.2_spmd.sunk.clone | while | flops 134742016 | bytes 3539513 | solution.py:110
  152.1 8.7 %select_reduce_fusion.1 = f32[2,4,256]{2,1,0:T(4,128)S(1)} fusion(f32[9,2,4,256,256]{3,4,2,1,0:T(8,128)} %get-tuple-element.354, pred[9,256,256]{1,2,0:T(8,128)(4,1)S(1)} %copy.180), kind=kLoop, calls=%fused_computation.20 | loop fusion | flops 9435136 | bytes 19472384 | tf_op jit(solution)/shard_map/reduce_max | solution.py:112
  160.8 9.6 %select_reduce_fusion = f32[2,4,256]{2,1,0:T(4,128)S(1)} fusion(f32[9,2,4,256,256]{3,4,2,1,0:T(8,128)} %get-tuple-element.354, f32[2,4,256]{2,1,0:T(4,128)S(1)} %select_reduce_fusion.1, pred[9,256,256]{1,2,0:T(8,128)(4,1)S(1)} %copy.180), kind=kLoop, calls=%fused_computation.19 | loop fusion | flops 14153728 | bytes 19480576 | tf_op jit(solution)/shard_map/reduce_sum | solution.py:113
  170.4 77.9 %while.27 = (s32[]{:T(128)}, f32[256,2,4,128]{0,3,2,1:T(8,128)}, bf16[9,256,512]{1,2,0:T(8,128)(2,1)}, pred[9,256,256]{2,1,0:T(8,128)(4,1)S(1)}, f32[9,2,4,256,256]{3,4,2,1,0:T(8,128)}, /*index=5*/f32[2,4,256]{2,1,0:T(4,128)S(1)}) while((s32[]{:T(128)}, f32[256,2,4,128]{0,3,2,1:T(8,128)}, ...), condition=%wide.region_6.7_spmd.clone.clone, body=%wide.region_5.6_spmd.clone.sunk.clone | while | flops 136314880 | bytes 13705307 | solution.py:136
  170.4 3.1 constant_dynamic-slice_fusion.7
  178.0 3.1 constant_dynamic-slice_fusion.7
  184.0 2.8 fusion.238
  186.8 3.1 constant_dynamic-slice_fusion.7
  192.8 2.8 fusion.238
  195.6 3.1 constant_dynamic-slice_fusion.7
  201.6 2.8 fusion.238
  204.4 3.1 constant_dynamic-slice_fusion.7
  210.4 2.8 fusion.238
  213.2 3.1 constant_dynamic-slice_fusion.7
  219.2 2.8 fusion.238
  221.9 3.1 constant_dynamic-slice_fusion.7
  227.9 2.8 fusion.238
  230.7 3.1 constant_dynamic-slice_fusion.7
  236.7 2.8 fusion.238
  239.5 3.1 constant_dynamic-slice_fusion.7
  245.5 2.8 fusion.238
  248.3 2.4 fusion.92
  260.0 2.8 fusion.69
  268.4 26.4 %collective-permute-start.11 = (bf16[256,512]{1,0:T(8,128)(2,1)}, bf16[256,512]{1,0:T(8,128)(2,1)}, u32[]{:S(2)}, u32[]{:S(2)}) collective-permute-start(bf16[256,512]{1,0:T(8,128)(2,1)} %pad_maximum_fusion.3), channel_id=1, source_target_pairs={{4,0},{6,2},{8,4},{10,6},{12,8},{14,10},{16,12},{18,14},{20,16},{2... | collective-permute-start | bytes 786440 | tf_op jit(solution)/shard_map/ppermute | solution.py:33
  304.8 2.3 collective-permute-start.12
  319.7 2.8 fusion.75
  324.8 2.3 fusion.26
  332.9 2.8 fusion.77
  344.1 2.8 fusion.79
  355.4 2.8 fusion.81
  364.9 2.8 fusion.90
  387.9 17.6 %collective-permute-done.15 = bf16[256,512]{1,0:T(8,128)(2,1)S(1)} collective-permute-done((bf16[256,512]{1,0:T(8,128)(2,1)}, bf16[256,512]{1,0:T(8,128)(2,1)S(1)}, u32[]{:S(2)}, u32[]{:S(2)}) %collective-permute-start.15) | collective-permute-done | bytes 262176 | tf_op jit(solution)/shard_map/ppermute | solution.py:33
  405.5 5.6 %collective-permute-done.16 = bf16[256,512]{1,0:T(8,128)(2,1)S(1)} collective-permute-done((bf16[256,512]{1,0:T(8,128)(2,1)}, bf16[256,512]{1,0:T(8,128)(2,1)S(1)}, u32[]{:S(2)}, u32[]{:S(2)}) %collective-permute-start.16) | collective-permute-done | bytes 262176 | tf_op jit(solution)/shard_map/ppermute | solution.py:33
  411.1 5.6 %collective-permute-done.17 = bf16[256,512]{1,0:T(8,128)(2,1)S(1)} collective-permute-done((bf16[256,512]{1,0:T(8,128)(2,1)}, bf16[256,512]{1,0:T(8,128)(2,1)S(1)}, u32[]{:S(2)}, u32[]{:S(2)}) %collective-permute-start.17) | collective-permute-done | bytes 262176 | tf_op jit(solution)/shard_map/ppermute | solution.py:33
  (308 shorter events, 202.1 us)
Async XLA Ops:
  0.6 18.5 %copy-start.23 = (bf16[128,2048]{1,0:T(8,128)(2,1)S(1)}, bf16[128,2048]{1,0:T(8,128)(2,1)}, u32[]{:S(2)}) copy-start(bf16[128,2048]{1,0:T(8,128)(2,1)} %param.10) | copy-start | bytes 1572868
  0.6 19.4 %copy-start.41 = (s32[32]{0:T(128)S(1)}, s32[32]{0:T(128)}, u32[]{:S(2)}) copy-start(s32[32]{0:T(128)} %param.15) | copy-start | bytes 388
  2.3 6.7 %all-to-all-start.1 = ((bf16[128,2,256]{2,0,1:T(8,128)(2,1)}), bf16[128,2,256]{2,0,1:T(8,128)(2,1)S(1)}, u32[]{:S(2)}, u32[]{:S(2)}) async-start(bf16[128,2,256]{2,0,1:T(8,128)(2,1)} %bitcast.573), calls=%async_computation.1 | async-start | bytes 262144 | tf_op jit(solution)/shard_map/all_to_all | solution.py:40
  9.0 6.7 %all-to-all-start.2 = ((bf16[128,2,256]{2,0,1:T(8,128)(2,1)}), bf16[128,2,256]{2,0,1:T(8,128)(2,1)S(1)}, u32[]{:S(2)}, u32[]{:S(2)}) async-start(bf16[128,2,256]{2,0,1:T(8,128)(2,1)} %bitcast.572), calls=%async_computation.2 | async-start | bytes 262144 | tf_op jit(solution)/shard_map/all_to_all | solution.py:41
  12.4 15.9 %copy-start.42 = (s32[32]{0:T(128)S(1)}, s32[32]{0:T(128)}, u32[]{:S(2)}) copy-start(s32[32]{0:T(128)} %param.14) | copy-start | bytes 388
  15.7 8.9 %all-to-all-start.3 = ((bf16[128,2,1024]{2,0,1:T(8,128)(2,1)}), bf16[128,2,1024]{2,0,1:T(8,128)(2,1)S(1)}, u32[]{:S(2)}, u32[]{:S(2)}) async-start(bf16[128,2,1024]{2,0,1:T(8,128)(2,1)} %bitcast.570), calls=%async_computation.3 | async-start | bytes 1048576 | tf_op jit(solution)/shard_map/all_to_all | solution.py:42
  24.6 8.9 %all-to-all-start = ((bf16[128,2,1024]{2,0,1:T(8,128)(2,1)}), bf16[128,2,1024]{2,0,1:T(8,128)(2,1)S(1)}, u32[]{:S(2)}, u32[]{:S(2)}) async-start(bf16[128,2,1024]{2,0,1:T(8,128)(2,1)} %bitcast.571), calls=%async_computation | async-start | bytes 1048576 | tf_op jit(solution)/shard_map/all_to_all | solution.py:39
  34.6 37.2 %collective-permute-start = (bf16[256,2560]{1,0:T(8,128)(2,1)}, bf16[256,2560]{1,0:T(8,128)(2,1)}, u32[]{:S(2)}, u32[]{:S(2)}) collective-permute-start(bf16[256,2560]{1,0:T(8,128)(2,1)} %pad_maximum_fusion.1), channel_id=1, source_target_pairs={{0,2},{2,4},{4,6},{6,8},{8,10},{10,12},{12,14},{14,16},{16,18},{18... | collective-permute-start | bytes 3932168 | tf_op jit(solution)/shard_map/ppermute | solution.py:21
  42.9 30.5 %collective-permute-start.1 = (bf16[256,2560]{1,0:T(8,128)(2,1)}, bf16[256,2560]{1,0:T(8,128)(2,1)}, u32[]{:S(2)}, u32[]{:S(2)}) collective-permute-start(bf16[256,2560]{1,0:T(8,128)(2,1)} %pad_maximum_fusion.1), channel_id=1, source_target_pairs={{2,0},{4,2},{6,4},{8,6},{10,8},{12,10},{14,12},{16,14},{18,16},{20... | collective-permute-start | bytes 3932168 | tf_op jit(solution)/shard_map/ppermute | solution.py:23
  48.6 211.4 %copy-start.40 = (pred[256,256]{0,1:T(8,128)(4,1)}, pred[256,256]{0,1:T(8,128)(4,1)S(1)}, u32[]{:S(2)}) copy-start(pred[256,256]{0,1:T(8,128)(4,1)S(1)} %copy.191) | copy-start | bytes 196612
  83.2 18.2 %collective-permute-start.2 = (bf16[256,512]{0,1:T(8,128)(2,1)}, bf16[256,512]{0,1:T(8,128)(2,1)}, u32[]{:S(2)}, u32[]{:S(2)}) collective-permute-start(bf16[256,512]{0,1:T(8,128)(2,1)} %copy.360), channel_id=1, source_target_pairs={{0,2},{2,4},{4,6},{6,8},{8,10},{10,12},{12,14},{14,16},{16,18},{18... | collective-permute-start | bytes 786440 | tf_op jit(solution)/shard_map/ppermute | solution.py:33
  86.0 19.0 %collective-permute-start.3 = (bf16[256,512]{0,1:T(8,128)(2,1)}, bf16[256,512]{0,1:T(8,128)(2,1)}, u32[]{:S(2)}, u32[]{:S(2)}) collective-permute-start(bf16[256,512]{0,1:T(8,128)(2,1)} %copy.360), channel_id=1, source_target_pairs={{0,4},{2,6},{4,8},{6,10},{8,12},{10,14},{12,16},{14,18},{16,20},{1... | collective-permute-start | bytes 786440 | tf_op jit(solution)/shard_map/ppermute | solution.py:33
  88.0 20.0 %collective-permute-start.4 = (bf16[256,512]{0,1:T(8,128)(2,1)}, bf16[256,512]{0,1:T(8,128)(2,1)}, u32[]{:S(2)}, u32[]{:S(2)}) collective-permute-start(bf16[256,512]{0,1:T(8,128)(2,1)} %copy.360), channel_id=1, source_target_pairs={{0,6},{2,8},{4,10},{6,12},{8,14},{10,16},{12,18},{14,20},{16,22},{... | collective-permute-start | bytes 786440 | tf_op jit(solution)/shard_map/ppermute | solution.py:33
  90.7 20.5 %collective-permute-start.5 = (bf16[256,512]{0,1:T(8,128)(2,1)}, bf16[256,512]{0,1:T(8,128)(2,1)}, u32[]{:S(2)}, u32[]{:S(2)}) collective-permute-start(bf16[256,512]{0,1:T(8,128)(2,1)} %copy.360), channel_id=1, source_target_pairs={{0,8},{2,10},{4,12},{6,14},{8,16},{10,18},{12,20},{14,22},{16,24},... | collective-permute-start | bytes 786440 | tf_op jit(solution)/shard_map/ppermute | solution.py:33
  92.6 20.2 %collective-permute-start.6 = (bf16[256,512]{0,1:T(8,128)(2,1)}, bf16[256,512]{0,1:T(8,128)(2,1)S(1)}, u32[]{:S(2)}, u32[]{:S(2)}) collective-permute-start(bf16[256,512]{0,1:T(8,128)(2,1)} %copy.360), channel_id=1, source_target_pairs={{0,10},{2,12},{4,14},{6,16},{8,18},{10,20},{12,22},{14,24},{16,26}... | collective-permute-start | bytes 786440 | tf_op jit(solution)/shard_map/ppermute | solution.py:33
  101.5 18.3 %collective-permute-start.7 = (bf16[256,512]{0,1:T(8,128)(2,1)}, bf16[256,512]{0,1:T(8,128)(2,1)S(1)}, u32[]{:S(2)}, u32[]{:S(2)}) collective-permute-start(bf16[256,512]{0,1:T(8,128)(2,1)} %copy.360), channel_id=1, source_target_pairs={{0,12},{2,14},{4,16},{6,18},{8,20},{10,22},{12,24},{14,26},{16,28}... | collective-permute-start | bytes 786440 | tf_op jit(solution)/shard_map/ppermute | solution.py:33
  105.0 20.2 %collective-permute-start.8 = (bf16[256,512]{0,1:T(8,128)(2,1)}, bf16[256,512]{0,1:T(8,128)(2,1)S(1)}, u32[]{:S(2)}, u32[]{:S(2)}) collective-permute-start(bf16[256,512]{0,1:T(8,128)(2,1)} %copy.360), channel_id=1, source_target_pairs={{0,14},{2,16},{4,18},{6,20},{8,22},{10,24},{12,26},{14,28},{16,30}... | collective-permute-start | bytes 786440 | tf_op jit(solution)/shard_map/ppermute | solution.py:33
  108.0 18.0 %collective-permute-start.9 = (bf16[256,512]{0,1:T(8,128)(2,1)}, bf16[256,512]{0,1:T(8,128)(2,1)S(1)}, u32[]{:S(2)}, u32[]{:S(2)}) collective-permute-start(bf16[256,512]{0,1:T(8,128)(2,1)} %copy.360), channel_id=1, source_target_pairs={{0,16},{2,18},{4,20},{6,22},{8,24},{10,26},{12,28},{14,30},{1,17},... | collective-permute-start | bytes 786440 | tf_op jit(solution)/shard_map/ppermute | solution.py:33
  112.8 14.0 %copy-start.16 = (bf16[256,512]{0,1:T(8,128)(2,1)}, bf16[256,512]{0,1:T(8,128)(2,1)S(1)}, u32[]{:S(2)}) copy-start(bf16[256,512]{0,1:T(8,128)(2,1)S(1)} %collective-permute-done.6) | copy-start | bytes 786436
  119.7 7.0 %copy-start.20 = (bf16[256,512]{0,1:T(8,128)(2,1)}, bf16[256,512]{0,1:T(8,128)(2,1)S(1)}, u32[]{:S(2)}) copy-start(bf16[256,512]{0,1:T(8,128)(2,1)S(1)} %collective-permute-done.7) | copy-start | bytes 786436
  248.3 2.4 copy-start.12
  258.1 122.6 %collective-permute-start.10 = (bf16[256,512]{1,0:T(8,128)(2,1)}, bf16[256,512]{1,0:T(8,128)(2,1)}, u32[]{:S(2)}, u32[]{:S(2)}) collective-permute-start(bf16[256,512]{1,0:T(8,128)(2,1)} %pad_maximum_fusion.2), channel_id=1, source_target_pairs={{2,0},{4,2},{6,4},{8,6},{10,8},{12,10},{14,12},{16,14},{18,16},{20... | collective-permute-start | bytes 786440 | tf_op jit(solution)/shard_map/ppermute | solution.py:33
  268.4 114.3 %collective-permute-start.11 = (bf16[256,512]{1,0:T(8,128)(2,1)}, bf16[256,512]{1,0:T(8,128)(2,1)}, u32[]{:S(2)}, u32[]{:S(2)}) collective-permute-start(bf16[256,512]{1,0:T(8,128)(2,1)} %pad_maximum_fusion.3), channel_id=1, source_target_pairs={{4,0},{6,2},{8,4},{10,6},{12,8},{14,10},{16,12},{18,14},{20,16},{2... | collective-permute-start | bytes 786440 | tf_op jit(solution)/shard_map/ppermute | solution.py:33
  304.8 6.8 %copy-start.39 = (pred[256,256]{0,1:T(8,128)(4,1)S(1)}, pred[256,256]{0,1:T(8,128)(4,1)}, u32[]{:S(2)}) copy-start(pred[256,256]{0,1:T(8,128)(4,1)} %copy.199) | copy-start | bytes 196612
  304.8 79.2 %collective-permute-start.12 = (bf16[256,512]{1,0:T(8,128)(2,1)}, bf16[256,512]{1,0:T(8,128)(2,1)}, u32[]{:S(2)}, u32[]{:S(2)}) collective-permute-start(bf16[256,512]{1,0:T(8,128)(2,1)} %pad_maximum_fusion.4), channel_id=1, source_target_pairs={{6,0},{8,2},{10,4},{12,6},{14,8},{16,10},{18,12},{20,14},{22,16},{... | collective-permute-start | bytes 786440 | tf_op jit(solution)/shard_map/ppermute | solution.py:33
  316.0 8.1 %copy-start.17 = (bf16[256,512]{0,1:T(8,128)(2,1)S(1)}, bf16[256,512]{0,1:T(8,128)(2,1)}, u32[]{:S(2)}) copy-start(bf16[256,512]{0,1:T(8,128)(2,1)} %copy-done.16) | copy-start | bytes 786436
  317.8 70.1 %collective-permute-start.13 = (bf16[256,512]{1,0:T(8,128)(2,1)}, bf16[256,512]{1,0:T(8,128)(2,1)}, u32[]{:S(2)}, u32[]{:S(2)}) collective-permute-start(bf16[256,512]{1,0:T(8,128)(2,1)} %pad_maximum_fusion.5), channel_id=1, source_target_pairs={{8,0},{10,2},{12,4},{14,6},{16,8},{18,10},{20,12},{22,14},{24,16},... | collective-permute-start | bytes 786440 | tf_op jit(solution)/shard_map/ppermute | solution.py:33
  329.3 8.1 %copy-start.21 = (bf16[256,512]{0,1:T(8,128)(2,1)S(1)}, bf16[256,512]{0,1:T(8,128)(2,1)}, u32[]{:S(2)}) copy-start(bf16[256,512]{0,1:T(8,128)(2,1)} %copy-done.20) | copy-start | bytes 786436
  331.0 56.9 %collective-permute-start.14 = (bf16[256,512]{1,0:T(8,128)(2,1)}, bf16[256,512]{1,0:T(8,128)(2,1)}, u32[]{:S(2)}, u32[]{:S(2)}) collective-permute-start(bf16[256,512]{1,0:T(8,128)(2,1)} %pad_maximum_fusion.6), channel_id=1, source_target_pairs={{10,0},{12,2},{14,4},{16,6},{18,8},{20,10},{22,12},{24,14},{26,16}... | collective-permute-start | bytes 786440 | tf_op jit(solution)/shard_map/ppermute | solution.py:33
  342.4 6.1 %copy-start.19 = (bf16[256,512]{0,1:T(8,128)(2,1)S(1)}, bf16[256,512]{0,1:T(8,128)(2,1)}, u32[]{:S(2)}) copy-start(bf16[256,512]{0,1:T(8,128)(2,1)} %copy-done.18) | copy-start | bytes 786436
  353.7 6.1 %copy-start.15 = (bf16[256,512]{0,1:T(8,128)(2,1)S(1)}, bf16[256,512]{0,1:T(8,128)(2,1)}, u32[]{:S(2)}) copy-start(bf16[256,512]{0,1:T(8,128)(2,1)} %copy-done.14) | copy-start | bytes 786436
  364.2 3.6 copy-start.37
  364.9 2.8 copy-start.38
  370.0 2.2 copy-start.22
  371.1 2.9 copy-start.25
  372.3 3.3 copy-start.3
  372.3 3.3 copy-start.26
  374.0 2.0 copy-start.5
  374.0 2.0 copy-start.27
  376.9 1.7 copy-start.33
  377.2 2.1 copy-start.35
  377.2 2.1 copy-start.36
  377.2 2.8 copy-start.24
  378.6 1.8 copy-start.9
  378.6 1.8 copy-start.29
  380.7 24.8 %collective-permute-start.15 = (bf16[256,512]{1,0:T(8,128)(2,1)}, bf16[256,512]{1,0:T(8,128)(2,1)S(1)}, u32[]{:S(2)}, u32[]{:S(2)}) collective-permute-start(bf16[256,512]{1,0:T(8,128)(2,1)} %pad_maximum_fusion.7), channel_id=1, source_target_pairs={{12,0},{14,2},{16,4},{18,6},{20,8},{22,10},{24,12},{26,14},{28,16}... | collective-permute-start | bytes 786440 | tf_op jit(solution)/shard_map/ppermute | solution.py:33
  382.7 28.5 %collective-permute-start.16 = (bf16[256,512]{1,0:T(8,128)(2,1)}, bf16[256,512]{1,0:T(8,128)(2,1)S(1)}, u32[]{:S(2)}, u32[]{:S(2)}) collective-permute-start(bf16[256,512]{1,0:T(8,128)(2,1)} %pad_maximum_fusion.8), channel_id=1, source_target_pairs={{14,0},{16,2},{18,4},{20,6},{22,8},{24,10},{26,12},{28,14},{30,16}... | collective-permute-start | bytes 786440 | tf_op jit(solution)/shard_map/ppermute | solution.py:33
  384.0 32.8 %collective-permute-start.17 = (bf16[256,512]{1,0:T(8,128)(2,1)}, bf16[256,512]{1,0:T(8,128)(2,1)S(1)}, u32[]{:S(2)}, u32[]{:S(2)}) collective-permute-start(bf16[256,512]{1,0:T(8,128)(2,1)} %pad_maximum_fusion.9), channel_id=1, source_target_pairs={{16,0},{18,2},{20,4},{22,6},{24,8},{26,10},{28,12},{30,14},{17,1},... | collective-permute-start | bytes 786440 | tf_op jit(solution)/shard_map/ppermute | solution.py:33
  (17 other events, 19.8 us)
where the time goes:
time: 428 us; the launch traced here: 420 us
  local copies, waits for them, and re-layouts  136 us (32%)
  matrix products  95.4 us (22%)
  starting transfers between devices  78.8 us (18%)
  waiting for transfers between devices  71.2 us (17%)
  other arithmetic  36.6 us (9%)
    ppermute x16, starting transfers between devices, passed_along(): return lax.ppermute(block, axis, route)  54.9 us
    dynamic_slice x18, local copies, waits for them, and re-layouts, per_device(): lax.scan(second_pass, out_start, (stacked, visible_all, scores_all))  44.8 us
    ppermute x16, waiting for transfers between devices, passed_along(): return lax.ppermute(block, axis, route)  39.8 us
    dot_general x9, matrix products, second_pass(): jnp.einsum('gqtu,ugd->tgqd', probability_lowered, local_values, preferred...  23.9 us
    dot_general x9, matrix products, gradients(): jnp.einsum('nzev,enzx->vnx', probability_lowered, grad_four, preferred_el...  22.9 us
    unnamed x103, local copies, waits for them, and re-layouts  22.8 us
    dot_general x9, matrix products, gradients(): jnp.einsum('tgqd,ugd->gqtu', grad_four, local_values, preferred_element_t...  20.3 us
    ppermute x1, waiting for transfers between devices, with_halo(): lax.ppermute(tail, axis, [(i, (i + 1) % count) for i in range(ends)])  17.9 us
  transfers between devices with their start and end apart: 22, of which 11 were waited for; matrix products, arithmetic and copies ran while one was open for 27% of the time, Pallas kernels for 0%

commit v1 on v0

v1 whole, which is shorter than its diff:
```python
import functools
import math

import jax
import jax.numpy as jnp
from jax import lax
from jax.experimental import pallas as pl
from jax.experimental.pallas import tpu as pltpu
from jax.sharding import PartitionSpec as P

BLK = 128
WINDOW = 2048
HEAD = 128
ROOT = 1.0 / math.sqrt(HEAD)
EXP2_SCALE = ROOT * math.log2(math.e)
HIDDEN = -1e30
NN = (((1,), (0,)), ((), ()))
TN = (((0,), (0,)), ((), ()))
SAFE_TOTAL = 2.0**60
SIDES = 2
BACK = 4
CHUNKS = SIDES * (BACK + 1)
SPLIT = 2 * SIDES
FLIPS = ((0, 0), (0, 1), (1, 0), (1, 1))
VMEM = pl.BlockSpec(memory_space=pltpu.VMEM)
SMEM = pl.BlockSpec(memory_space=pltpu.SMEM)
ANY = pl.BlockSpec(memory_space=pl.ANY)
SMALL = pltpu.CompilerParams(vmem_limit_bytes=8 * 1024 * 1024)
def dot(a, b, dims):
    return lax.dot_general(a, b, dims, preferred_element_type=jnp.float32)


def position():
    seq_at = lax.axis_index("seq")
    return seq_at // SIDES, seq_at % SIDES, lax.axis_index("head")


def local_slots(chip_at, core_at, head_at):
    return [
        SIDES * 2 * chip_at + 2 * (core_at ^ core_flip) + (head_at ^ head_flip)
        for core_flip, head_flip in FLIPS
    ]


def turned(array):
    return jnp.transpose(array.astype(jnp.float32))


def pack_kernel(width, one, two, p0, p1, p2, p3, landed, sems):
    copies = [
        pltpu.make_async_copy(ref, landed.at[which], sems.at[which])
        for which, ref in enumerate((one, two))
    ]
    for copy in copies:
        copy.start()
    for copy in copies:
        copy.wait()
    unused, core_at, head_at = position()
    for target, (core_flip, head_flip) in zip((p0, p1, p2, p3), FLIPS):
        group = SIDES * (head_at ^ head_flip) + (core_at ^ core_flip)
        columns = pl.ds(pl.multiple_of(group * width, width), width)
        for which in range(2):
            target[:, which * width : (which + 1) * width] = landed[which, :, columns]


def pack(one, two, groups):
    rows, columns = one.shape
    width = columns // groups
    packet = jax.ShapeDtypeStruct((rows, 2 * width), jnp.bfloat16)
    return pl.pallas_call(
        functools.partial(pack_kernel, width),
        out_shape=[packet] * 4,
        in_specs=[ANY] * 2,
        out_specs=[VMEM] * 4,
        scratch_shapes=[
            pltpu.VMEM((2, rows, columns), jnp.bfloat16),
            pltpu.SemaphoreType.DMA((2,)),
        ],
        compiler_params=SMALL,
        cost_estimate=pl.CostEstimate(flops=0, bytes_accessed=8 * rows * columns, transcendentals=0),
    )(one, two)


def move_kernel(home, q0, q1, q2, q3, k0, k1, k2, k3, right, left):
    chip_at, core_at, head_at = position()
    width = q0.shape[1]
    for slot, q, k in zip(local_slots(chip_at, core_at, head_at), (q0, q1, q2, q3), (k0, k1, k2, k3)):
        target = home[slot] // (2 * SIDES)

        @pl.when(target > chip_at)
        def _():
            right[...] = q[...]

        @pl.when(target < chip_at)
        def _():
            left[:, :width] = q[...]
            left[:, width:] = k[...]


def movers(home, queries, keys):
    rows, width = queries[0].shape
    return pl.pallas_call(
        move_kernel,
        out_shape=[
            jax.ShapeDtypeStruct((rows, width), jnp.bfloat16),
            jax.ShapeDtypeStruct((rows, width + keys[0].shape[1]), jnp.bfloat16),
        ],
        in_specs=[SMEM] + [VMEM] * 8,
        out_specs=[VMEM] * 2,
        compiler_params=SMALL,
        cost_estimate=pl.CostEstimate(flops=0, bytes_accessed=8 * rows * width, transcendentals=0),
    )(home, *queries, *keys)


def end_kernel(home, k0, k1, k2, k3, right):
    chip_at, core_at, head_at = position()
    for slot, ref in zip(local_slots(chip_at, core_at, head_at), (k0, k1, k2, k3)):
        @pl.when(home[slot] // (2 * SIDES) > chip_at)
        def _():
            right[...] = ref[...]


def key_mover(home, keys):
    return pl.pallas_call(
        end_kernel,
        out_shape=jax.ShapeDtypeStruct(keys[0].shape, jnp.bfloat16),
        in_specs=[SMEM] + [VMEM] * 4,
        out_specs=VMEM,
        compiler_params=SMALL,
        cost_estimate=pl.CostEstimate(
            flops=0, bytes_accessed=8 * keys[0].size, transcendentals=0
        ),
    )(home, *keys)


def block_sources(home, chip_at, core_at, head_at, b):
    slots = local_slots(chip_at, core_at, head_at)
    before = jnp.maximum(2 * SIDES * (chip_at - 1), 0)
    block = 2 * SIDES * chip_at + b
    here = [home[slot] == block for slot in slots]
    from_left = home[before] == block
    for other in range(1, 2 * SIDES):
        from_left = from_left | (home[before + other] == block)
    outside = jnp.logical_not(here[0] | here[1] | here[2] | here[3])
    return here + [outside & from_left, outside & jnp.logical_not(from_left)]


def key_ranges(docs, chip_at):
    first = SIDES * (chip_at - BACK)

    def doc_at(j, half):
        return docs[jnp.maximum(2 * (first + j) + half, 0)]

    limit = [SIDES * BACK + i + 1 for i in range(SIDES)]
    lowest = []
    for i in range(SIDES):
        own = SIDES * BACK + i
        low = jnp.int32(own)
        for j in range(i, own):
            alike = (first + j >= 0) & (doc_at(j, 1) == doc_at(own, 0))
            low = low - alike.astype(jnp.int32)
        lowest.append(low)
    return doc_at, lowest, limit, jnp.minimum(lowest[0], lowest[1])


def gradient_loop(
    per_group, tokens, lowest, limit, start, stop, outputs,
    kv, values_turned, e_low, spread, q_stack, do_stack, dq, ds_low,
):
    def chunk(j):
        return pl.ds(pl.multiple_of(j * tokens, tokens), tokens)

    def store(j, value):
        for back, ref in outputs.items():
            @pl.when(j // SIDES == BACK - back)
            def _():
                ref[j % SIDES] = value

    def grad_terms(i, j):
        value_term = dot(e_low[i, j - i], do_stack[i], TN)
        key_term = None
        for h in range(per_group):
            rows = slice(h * tokens, (h + 1) * tokens)
            delta = spread[i, rows]
            dp = dot(do_stack[i, rows], values_turned[j], NN)
            e = e_low[i, j - i, rows].astype(jnp.float32)
            g0 = e[:, :HEAD] * (dp[:, :HEAD] - delta)
            g1 = e[:, HEAD:] * (dp[:, HEAD:] - delta)
            ds = jnp.concatenate([g0, g1], axis=1).astype(jnp.bfloat16)
            ds_low[i, rows] = ds
            dq[i, rows] += dot(ds, kv[chunk(j), :HEAD], NN)
            if h % 2 == 1:
                part = slice((h - 1) * tokens, (h + 1) * tokens)
                term = dot(ds_low[i, part], q_stack[i, part], TN)
                key_term = term if key_term is None else key_term + term
        return jnp.concatenate([key_term * ROOT, value_term], axis=1)

    def grad_pass(j, carry):
        inside = [(j >= lowest[i]) & (j < limit[i]) for i in range(SIDES)]

        @pl.when(inside[0] & inside[1])
        def _():
            store(j, (grad_terms(0, j) + grad_terms(1, j)).astype(jnp.bfloat16))

        for i in range(SIDES):
            @pl.when(inside[i] & jnp.logical_not(inside[1 - i]))
            def _():
                store(j, grad_terms(i, j).astype(jnp.bfloat16))

        return carry

    def no_terms(j, carry):
        store(j, jnp.zeros((tokens, 2 * HEAD), jnp.bfloat16))
        return carry

    begin = jnp.clip(jnp.minimum(lowest[0], lowest[1]), start, stop)
    lax.fori_loop(start, begin, no_terms, 0)
    lax.fori_loop(begin, stop, grad_pass, 0)


def attention_kernel(
    per_group, tokens, shards,
    docs, home, b0, b1, b2, b3, b4, b5, c0, c1, c2, c3, c4, end_far,
    keep, send, d3, d4, kv, values_turned, e_low, spread, q_stack, do_stack, dq,
    ones, keys_turned, top, acc, ds_low, landed, end_near, sems,
):
    chip_at, core_at, head_at = position()
    q_width = per_group * HEAD

    def land(ref, b):
        return pltpu.make_async_copy(ref.at[:, pl.ds(0, 2 * q_width)], landed.at[b], sems.at[b])

    end_copy = pltpu.make_async_copy(
        b5.at[:, pl.ds(2 * q_width, 2 * HEAD)], end_near, sems.at[2 * SIDES]
    )
    end_copy.start()

    for b in range(2 * SIDES):
        flags = block_sources(home, chip_at, core_at, head_at, b)
        for flag, ref in zip(flags, (b0, b1, b2, b3, b4, b5)):
            @pl.when(flag)
            def _():
                land(ref, b).start()

    chip_blocks = 2 * SIDES
    window = chip_blocks * (chip_at - BACK)

    def write_key_block(block, known, value):
        place = block - window

        @pl.when(known & (place >= 0) & (place < chip_blocks * (BACK + 1)))
        def _():
            rows = pl.ds(pl.multiple_of(place * BLK, BLK), BLK)
            kv[rows] = value[...]
            ones[rows, :HEAD] = value[:, HEAD:]
            ones[rows, HEAD:] = jnp.ones((BLK, HEAD), jnp.bfloat16)

    def write_chip(back, ref):
        known = chip_at >= back
        for which, slot in enumerate(local_slots(chip_at - back, core_at, head_at)):
            write_key_block(home[jnp.maximum(slot, 0)], known, ref.at[which])

    def write_end(chip, target, ref):
        known = (chip >= 0) & (chip < shards // SIDES)
        slot = jnp.where(known, chip_blocks * chip, 0)
        for other in range(chip_blocks):
            block = home[slot + other]
            write_key_block(block, known & (block // chip_blocks == target), ref)

    for back, ref in enumerate((c0, c1, c2, c3, c4)):
        write_chip(back, ref)
    write_end(chip_at - BACK - 1, chip_at - BACK, end_far)
    end_copy.wait()
    write_end(chip_at + 1, chip_at, end_near)
    for b in range(2 * SIDES):
        land(b0, b).wait()
        for h in range(per_group):
            rows = slice(h * tokens + (b % 2) * BLK, h * tokens + (b % 2 + 1) * BLK)
            q_stack[b // 2, rows] = landed[b, :, h * HEAD : (h + 1) * HEAD]
            do_stack[b // 2, rows] = landed[b, :, q_width + h * HEAD : q_width + (h + 1) * HEAD]

    def chunk(j):
        return pl.ds(pl.multiple_of(j * tokens, tokens), tokens)

    doc_at, lowest, limit, begin = key_ranges(docs, chip_at)

    row = lax.broadcasted_iota(jnp.int32, (tokens, tokens), 0)
    col = lax.broadcasted_iota(jnp.int32, (tokens, tokens), 1)

    def hidden(i, j):
        own = SIDES * BACK + i
        q_doc = jnp.where(row < BLK, doc_at(own, 0), doc_at(own, 1))
        k_doc = jnp.where(col < BLK, doc_at(j, 0), doc_at(j, 1))
        gap = row - col + (own - j) * tokens
        seen = (q_doc == k_doc) & (gap >= 0) & (gap < WINDOW)
        return jnp.where(seen, 0.0, HIDDEN)

    k_cols = slice(0, HEAD)
    v_cols = slice(HEAD, 2 * HEAD)

    def turn_chunk(j, carry):
        keys_turned[j] = turned(kv[chunk(j), k_cols]).astype(jnp.bfloat16)
        values_turned[j] = turned(kv[chunk(j), v_cols]).astype(jnp.bfloat16)
        return carry

    lax.fori_loop(begin, CHUNKS, turn_chunk, 0)

    def head_rows(h):
        return slice(h * tokens, (h + 1) * tokens)

    def in_range(i, j):
        return (j >= lowest[i]) & (j < limit[i])

    def is_open(i, j):
        own = SIDES * BACK + i
        return (
            in_range(i, j)
            & (doc_at(j, 0) == doc_at(own, 1))
            & (j < own)
            & (j > own - SIDES * BACK)
        )

    def take_top(i, start):
        top[i] = jnp.full_like(top[i], HIDDEN)

        def widen(j, carry):
            bias = hidden(i, j)
            for h in range(per_group):
                rows = head_rows(h)
                s = dot(q_stack[i, rows], keys_turned[j], NN) + bias
                top[i, rows] = jnp.maximum(top[i, rows], jnp.maximum(s[:, :HEAD], s[:, HEAD:]))
            return carry

        lax.fori_loop(start, limit[i], widen, 0)
        for h in range(per_group):
            rows = head_rows(h)
            top[i, rows] = jnp.broadcast_to(
                jnp.max(top[i, rows], axis=1, keepdims=True), (tokens, HEAD)
            )

    def forward(i, j, bias):
        for h in range(per_group):
            rows = head_rows(h)
            s = dot(q_stack[i, rows], keys_turned[j], NN)
            if bias is not None:
                s = s + bias
            m = top[i, rows]
            e0 = jnp.exp2((s[:, :HEAD] - m) * EXP2_SCALE)
            e1 = jnp.exp2((s[:, HEAD:] - m) * EXP2_SCALE)
            low = jnp.concatenate([e0, e1], axis=1).astype(jnp.bfloat16)
            e_low[i, j - i, rows] = low
            acc[i, rows] += dot(low, ones[chunk(j)], NN)

    def forward_pass(j, carry):
        open_all = is_open(0, j) & is_open(1, j)

        @pl.when(open_all)
        def _():
            for i in range(SIDES):
                forward(i, j, None)

        for i in range(SIDES):
            @pl.when(in_range(i, j) & jnp.logical_not(open_all))
            def _():
                forward(i, j, hidden(i, j))

        return carry

    def attempt(carry):
        tries, unused = carry
        for i in range(SIDES):
            take_top(i, jnp.where(tries == 0, SIDES * BACK + i, lowest[i]))
        acc[...] = jnp.zeros_like(acc)
        lax.fori_loop(begin, CHUNKS, forward_pass, 0)
        safe = jnp.min(jnp.where(acc[:, :, HEAD:] < SAFE_TOTAL, 1.0, 0.0))
        return tries + 1, (safe < 0.5).astype(jnp.int32)

    lax.while_loop(
        lambda carry: (carry[0] == 0) | ((carry[0] == 1) & (carry[1] == 1)),
        attempt,
        (jnp.int32(0), jnp.int32(0)),
    )

    for i in range(SIDES):
        for h in range(per_group):
            rows = head_rows(h)
            inverse = 1.0 / acc[i, rows, HEAD:]
            attended = (acc[i, rows, :HEAD] * inverse).astype(jnp.bfloat16)

            @pl.when(core_at == i)
            def _():
                keep[:, h * HEAD : (h + 1) * HEAD] = attended

            @pl.when(core_at != i)
            def _():
                send[:, h * HEAD : (h + 1) * HEAD] = attended

            shared = (do_stack[i, rows].astype(jnp.float32) * inverse).astype(jnp.bfloat16)
            do_stack[i, rows] = shared
            delta = jnp.sum(
                shared.astype(jnp.float32) * attended.astype(jnp.float32), axis=1, keepdims=True
            )
            spread[i, rows] = jnp.broadcast_to(delta, (tokens, HEAD))
    dq[...] = jnp.zeros_like(dq)

    gradient_loop(
        per_group, tokens, lowest, limit, 0, SPLIT, {3: d3, 4: d4},
        kv, values_turned, e_low, spread, q_stack, do_stack, dq, ds_low,
    )


def second_kernel(
    per_group, tokens,
    docs, kv, values_turned, e_low, spread, q_stack, do_stack, dq_first,
    keep, send, d0, d1, d2, dq, ds_low,
):
    chip_at, core_at, head_at = position()
    unused, lowest, limit, begin = key_ranges(docs, chip_at)
    dq[...] = dq_first[...]
    gradient_loop(
        per_group, tokens, lowest, limit, SPLIT, CHUNKS, {0: d0, 1: d1, 2: d2},
        kv, values_turned, e_low, spread, q_stack, do_stack, dq, ds_low,
    )
    for i in range(SIDES):
        for h in range(per_group):
            gradient = (dq[i, h * tokens : (h + 1) * tokens] * ROOT).astype(jnp.bfloat16)

            @pl.when(core_at == i)
            def _():
                keep[:, h * HEAD : (h + 1) * HEAD] = gradient

            @pl.when(core_at != i)
            def _():
                send[:, h * HEAD : (h + 1) * HEAD] = gradient


def per_device(queries, key_states, value_vector_rows, grad_output, doc_ids, block_home):
    seq_at = lax.axis_index("seq")
    shards = lax.axis_size("seq")
    heads = lax.axis_size("head")
    tokens = queries.shape[0] * heads
    groups = key_states.shape[1] // HEAD
    per_group = queries.shape[1] // key_states.shape[1]
    assert heads == 2 and groups == heads * SIDES and tokens == 2 * BLK
    assert WINDOW == tokens * SIDES * BACK and shards % (2 * SIDES) == 0
    core_at = seq_at % SIDES
    everyone = range(shards)

    def both(array, step, flip):
        pairs = [
            (s * heads + x, (s ^ step) * heads + (x ^ flip)) for s in everyone for x in range(heads)
        ]
        return lax.ppermute(array, ("seq", "head"), pairs)

    def along(array, step):
        pairs = [(s, s + step) for s in everyone if 0 <= s + step < shards]
        return lax.ppermute(array, "seq", pairs)

    def core_swap(array):
        return lax.ppermute(array, "seq", [(s, s ^ 1) for s in everyone])

    def exchange(packets):
        return [
            packets[0],
            both(packets[1], 0, 1),
            both(packets[2], 1, 0),
            both(packets[3], 1, 1),
        ]

    kv_packets = pack(key_states, value_vector_rows, groups)
    qd_packets = pack(queries, grad_output, groups)
    kv_local, qd_packets = lax.optimization_barrier((exchange(kv_packets), qd_packets))
    own = jnp.stack(kv_local)
    qd_local = exchange(qd_packets)
    two_back = along(own, 2 * SIDES)
    one_back = along(own, SIDES)
    three_back = along(own, 3 * SIDES)
    kv_right = key_mover(block_home, kv_local)
    right, left = movers(block_home, qd_local, kv_local)
    right, left, one_back, two_back = lax.optimization_barrier((right, left, one_back, two_back))
    qd_all = qd_local + [along(right, SIDES), along(left, -SIDES)]
    four_back = along(two_back, 2 * SIDES)
    three_back, kv_right = lax.optimization_barrier((three_back, kv_right))
    end_far = along(kv_right, SIDES * (BACK + 1))

    rows = per_group * tokens
    q_width = per_group * HEAD
    pair_shape = jax.ShapeDtypeStruct((SIDES, tokens, 2 * HEAD), jnp.bfloat16)
    kept_shape = jax.ShapeDtypeStruct((tokens, q_width), jnp.bfloat16)
    state = [
        jax.ShapeDtypeStruct((CHUNKS * tokens, 2 * HEAD), jnp.bfloat16),
        jax.ShapeDtypeStruct((CHUNKS, HEAD, tokens), jnp.bfloat16),
        jax.ShapeDtypeStruct((SIDES, CHUNKS - 1, rows, tokens), jnp.bfloat16),
        jax.ShapeDtypeStruct((SIDES, rows, HEAD), jnp.float32),
        jax.ShapeDtypeStruct((SIDES, rows, HEAD), jnp.bfloat16),
        jax.ShapeDtypeStruct((SIDES, rows, HEAD), jnp.bfloat16),
        jax.ShapeDtypeStruct((SIDES, rows, HEAD), jnp.float32),
    ]
    work = 12 * BACK * SIDES * rows * tokens * HEAD
    keep, send, d3, d4, *carried = pl.pallas_call(
        functools.partial(attention_kernel, per_group, tokens, shards),
        out_shape=[kept_shape] * 2 + [pair_shape] * 2 + state,
        in_specs=[SMEM] * 2 + [ANY] * 6 + [VMEM] * 6,
        out_specs=[VMEM] * (4 + len(state)),
        scratch_shapes=[
            pltpu.VMEM((CHUNKS * tokens, 2 * HEAD), jnp.bfloat16),
            pltpu.VMEM((CHUNKS, HEAD, tokens), jnp.bfloat16),
            pltpu.VMEM((SIDES, rows, HEAD), jnp.float32),
            pltpu.VMEM((SIDES, rows, 2 * HEAD), jnp.float32),
            pltpu.VMEM((SIDES, rows, tokens), jnp.bfloat16),
            pltpu.VMEM((2 * SIDES, BLK, 2 * q_width), jnp.bfloat16),
            pltpu.VMEM((BLK, 2 * HEAD), jnp.bfloat16),
            pltpu.SemaphoreType.DMA((2 * SIDES + 1,)),
        ],
        compiler_params=pltpu.CompilerParams(vmem_limit_bytes=34 * 1024 * 1024),
        cost_estimate=pl.CostEstimate(
            flops=work, bytes_accessed=8 * 1024 * 1024, transcendentals=work // (12 * HEAD)
        ),
    )(doc_ids, block_home, *qd_all, own, one_back, two_back, three_back, four_back, end_far)
    dq_keep, dq_send, d0, d1, d2 = pl.pallas_call(
        functools.partial(second_kernel, per_group, tokens),
        out_shape=[kept_shape] * 2 + [pair_shape] * 3,
        in_specs=[SMEM] + [VMEM] * len(state),
        out_specs=[VMEM] * 5,
        scratch_shapes=[
            pltpu.VMEM((SIDES, rows, HEAD), jnp.float32),
            pltpu.VMEM((SIDES, rows, tokens), jnp.bfloat16),
        ],
        compiler_params=pltpu.CompilerParams(vmem_limit_bytes=8 * 1024 * 1024),
        cost_estimate=pl.CostEstimate(
            flops=work, bytes_accessed=8 * 1024 * 1024, transcendentals=0
        ),
    )(doc_ids, *carried)

    def added(term, arrived):
        return term.astype(jnp.float32) + arrived.astype(jnp.float32)

    first_core = core_at == 0

    def halves(pair):
        return (
            jnp.where(first_core, pair[0], pair[1]).astype(jnp.bfloat16),
            jnp.where(first_core, pair[1], pair[0]).astype(jnp.bfloat16),
        )

    four_in = along(d4, -2 * SIDES)
    three_in = along(d3, -SIDES)
    one_in = along(d1, -SIDES)
    own_kept, own_sent = halves(added(d0, one_in))
    own_taken = core_swap(own_sent)
    near_kept, near_sent = halves(added(d2, three_in) + four_in.astype(jnp.float32))
    down = [(s, (s - 2 * SIDES) ^ 1) for s in everyone if s >= 2 * SIDES]
    mine_in = along(near_kept, -2 * SIDES)
    theirs_in = lax.ppermute(near_sent, "seq", down)

    def joined(part):
        kept, taken = part
        return jnp.where(
            first_core,
            jnp.concatenate([kept, taken], axis=1),
            jnp.concatenate([taken, kept], axis=1),
        )

    attended = joined((keep, core_swap(send)))
    grad_query = joined((dq_keep, core_swap(dq_send)))
    mine_in, theirs_in, attended, grad_query = lax.optimization_barrier(
        (mine_in, theirs_in, attended, grad_query)
    )
    mine = added(own_kept, mine_in).astype(jnp.bfloat16)
    theirs = added(own_taken, theirs_in).astype(jnp.bfloat16)
    return (
        attended,
        grad_query,
        joined((mine[:, :HEAD], theirs[:, :HEAD])),
        joined((mine[:, HEAD:], theirs[:, HEAD:])),
    )


def solution(mesh):
    split = P(("seq", "head"), None)
    placed = P("seq", "head")
    return jax.shard_map(
        per_device,
        mesh=mesh,
        in_specs=(split, split, split, split, P(), P()),
        out_specs=(placed, placed, placed, placed),
        check_vma=False,
    )
```

time: 428 us -> 94.6 us (0.22); the launches traced: 420 us -> 94.9 us
  local copies, waits for them, and re-layouts: 136 us -> 5.87 us
  matrix products: 95.4 us -> 0 us
  waiting for transfers between devices: 71.2 us -> 17.8 us
  starting transfers between devices: 78.8 us -> 39.8 us
  other arithmetic: 36.6 us -> 2.98 us
  Pallas kernels: 0 us -> 27.4 us
    dot_general x54 -> x0, matrix products: 95.4 us -> none  [the longest x9 23.9 us: second_pass(): jnp.einsum('gqtu,ugd->tgqd', probability_lowered, local_values, preferred...]
    dynamic_slice x19 -> x0, local copies, waits for them, and re-layouts: 44.8 us -> none  [the longest x18 44.8 us: per_device(): lax.scan(second_pass, out_start, (stacked, visible_all, scores_all))]
    ppermute x18 -> x21, waiting for transfers between devices: 59.2 us -> 17.8 us  [the longest x11 12.8 us: along(): return lax.ppermute(array, 'seq', pairs)]
    pallas_call x0 -> x6, Pallas kernels: none -> 27.4 us  [the longest x1 14.9 us: per_device(): pl.pallas_call(functools.partial(attention_kernel, per_group, tokens, sha...]
    ppermute x18 -> x21, starting transfers between devices: 65.1 us -> 39.8 us  [the longest x11 27.7 us: along(): return lax.ppermute(array, 'seq', pairs)]
    squeeze x37 -> x0, local copies, waits for them, and re-layouts: 23.5 us -> none  [the longest x18 17.5 us: per_device(): unused_one, scores_all = lax.scan(score_pass, 0, (stacked, visible_all))]
    reshape x19 -> x0, local copies, waits for them, and re-layouts: 17.7 us -> none  [the longest x9 9.69 us: gradients(): value_contribution = jnp.einsum('nzev,enzx->vnx', probability_lowered, gr...]
    unnamed x103 -> x14, local copies, waits for them, and re-layouts: 22.8 us -> 5.85 us
  transfers between devices with their start and end apart: 22 -> 21, of which waited for: 11 -> 5; matrix products, arithmetic and copies ran while one was open for 27% -> 2% of each run, Pallas kernels for 0% -> 13%
where the time goes in v1:
time: 94.6 us; the launch traced here: 94.9 us
  starting transfers between devices  39.8 us (42%)
  Pallas kernels  27.4 us (29%)
  waiting for transfers between devices  17.8 us (19%)
  local copies, waits for them, and re-layouts  5.87 us (6%)
  other arithmetic  2.98 us (3%)
    ppermute x11, starting transfers between devices, along(): return lax.ppermute(array, 'seq', pairs)  27.7 us
    pallas_call x1, Pallas kernels, per_device(): pl.pallas_call(functools.partial(attention_kernel, per_group, tokens, sha...  14.9 us
    ppermute x11, waiting for transfers between devices, along(): return lax.ppermute(array, 'seq', pairs)  12.8 us
    pallas_call x1, Pallas kernels, per_device(): pl.pallas_call(functools.partial(second_kernel, per_group, tokens), out_s...  9.97 us
    ppermute x3, starting transfers between devices, core_swap(): return lax.ppermute(array, 'seq', [(s, s ^ 1) for s in everyone])  6.01 us
    unnamed x14, local copies, waits for them, and re-layouts  5.85 us
    ppermute x6, starting transfers between devices, both(): return lax.ppermute(array, ('seq', 'head'), pairs)  4.24 us
    ppermute x6, waiting for transfers between devices, both(): return lax.ppermute(array, ('seq', 'head'), pairs)  3.16 us
  transfers between devices with their start and end apart: 21, of which 5 were waited for; matrix products, arithmetic and copies ran while one was open for 2% of the time, Pallas kernels for 13%

profile of v1, /device:TPU:17, one launch (start us, length us, event | category | flops | bytes accessed | tf_op | source)
XLA Modules:
  0.0 94.9 jit_solution(2483426441857675854)
XLA Ops:
  0.6 0.9 copy-done.2
  1.5 0.9 copy-done.3
  2.4 0.4 shard_map.93
  2.8 1.3 %collective-permute-start = (bf16[128,256]{1,0:T(8,128)(2,1)S(1)}, bf16[128,256]{1,0:T(8,128)(2,1)S(1)}, u32[]{:S(2)}, u32[]{:S(2)}) collective-permute-start(bf16[128,256]{1,0:T(8,128)(2,1)S(1)} %get-tuple-element.49), channel_id=1, source_target_pairs={{0,1},{1,0},{2,3},{3,2},{4,5},{5,4},{6,7},{7,6},{8,9},{9,8},{10,11... | collective-permute-start | bytes 196616 | tf_op jit(solution)/shard_map/ppermute | solution.py:453
  4.1 1.0 %collective-permute-start.1 = (bf16[128,256]{1,0:T(8,128)(2,1)S(1)}, bf16[128,256]{1,0:T(8,128)(2,1)S(1)}, u32[]{:S(2)}, u32[]{:S(2)}) collective-permute-start(bf16[128,256]{1,0:T(8,128)(2,1)S(1)} %get-tuple-element.50), channel_id=1, source_target_pairs={{0,2},{1,3},{2,0},{3,1},{4,6},{5,7},{6,4},{7,5},{8,10},{9,11},{10,... | collective-permute-start | bytes 196616 | tf_op jit(solution)/shard_map/ppermute | solution.py:453
  5.1 0.1 collective-permute-start.2
  5.2 1.0 %copy-done = bf16[128,2048]{1,0:T(8,128)(2,1)S(1)} copy-done((bf16[128,2048]{1,0:T(8,128)(2,1)S(1)}, bf16[128,2048]{1,0:T(8,128)(2,1)}, u32[]{:S(2)}) %copy-start) | copy-done | bytes 524312
  6.3 1.0 %copy-done.1 = bf16[128,2048]{1,0:T(8,128)(2,1)S(1)} copy-done((bf16[128,2048]{1,0:T(8,128)(2,1)S(1)}, bf16[128,2048]{1,0:T(8,128)(2,1)}, u32[]{:S(2)}) %copy-start.1) | copy-done | bytes 524312
  7.3 0.2 shard_map.94
  7.5 0.0 collective-permute-done.k1
  7.5 0.0 collective-permute-done.1.k2
  7.5 1.3 %collective-permute-done.2.k3 = bf16[128,256]{1,0:T(8,128)(2,1)S(1)} collective-permute-done((bf16[128,256]{1,0:T(8,128)(2,1)S(1)}, bf16[128,256]{1,0:T(8,128)(2,1)S(1)}, u32[]{:S(2)}, u32[]{:S(2)}) %collective-permute-start.2) | collective-permute-done | bytes 65568 | tf_op jit(solution)/shard_map/ppermute | solution.py:453
  8.8 1.0 %collective-permute-start.3 = (bf16[128,1024]{1,0:T(8,128)(2,1)S(1)}, bf16[128,1024]{1,0:T(8,128)(2,1)S(1)}, u32[]{:S(2)}, u32[]{:S(2)}) collective-permute-start(bf16[128,1024]{1,0:T(8,128)(2,1)S(1)} %get-tuple-element.57), channel_id=1, source_target_pairs={{0,1},{1,0},{2,3},{3,2},{4,5},{5,4},{6,7},{7,6},{8,9},{9,8},{10,11... | collective-permute-start | bytes 786440 | tf_op jit(solution)/shard_map/ppermute | solution.py:453
  9.7 0.3 collective-permute-start.4
  10.0 0.6 collective-permute-start.5
  10.7 3.1 %collective-permute-start.6 = (bf16[4,128,256]{2,1,0:T(8,128)(2,1)S(1)}, bf16[4,128,256]{2,1,0:T(8,128)(2,1)S(1)}, u32[]{:S(2)}, u32[]{:S(2)}) collective-permute-start(bf16[4,128,256]{2,1,0:T(8,128)(2,1)S(1)} %pad_maximum_fusion.c0), channel_id=1, source_target_pairs={{0,4},{2,6},{4,8},{6,10},{8,12},{10,14},{12,16},{14,18},{16,20},{1... | collective-permute-start | bytes 786440 | tf_op jit(solution)/shard_map/ppermute | solution.py:457
  13.8 3.2 %collective-permute-start.7 = (bf16[4,128,256]{2,1,0:T(8,128)(2,1)S(1)}, bf16[4,128,256]{2,1,0:T(8,128)(2,1)S(1)}, u32[]{:S(2)}, u32[]{:S(2)}) collective-permute-start(bf16[4,128,256]{2,1,0:T(8,128)(2,1)S(1)} %pad_maximum_fusion.c0), channel_id=1, source_target_pairs={{0,8},{2,10},{4,12},{6,14},{8,16},{10,18},{12,20},{14,22},{16,24},... | collective-permute-start | bytes 786440 | tf_op jit(solution)/shard_map/ppermute | solution.py:457
  17.0 0.0 collective-permute-done.3.q1.b1
  17.1 3.8 %collective-permute-start.10 = (bf16[4,128,256]{2,1,0:T(8,128)(2,1)S(1)}, bf16[4,128,256]{2,1,0:T(8,128)(2,1)S(1)}, u32[]{:S(2)}, u32[]{:S(2)}) collective-permute-start(bf16[4,128,256]{2,1,0:T(8,128)(2,1)S(1)} %pad_maximum_fusion.c0), channel_id=1, source_target_pairs={{0,12},{2,14},{4,16},{6,18},{8,20},{10,22},{12,24},{14,26},{16,28}... | collective-permute-start | bytes 786440 | tf_op jit(solution)/shard_map/ppermute | solution.py:457
  20.8 1.9 %collective-permute-done.5.q3.b3 = bf16[128,1024]{1,0:T(8,128)(2,1)S(1)} collective-permute-done((bf16[128,1024]{1,0:T(8,128)(2,1)S(1)}, bf16[128,1024]{1,0:T(8,128)(2,1)S(1)}, u32[]{:S(2)}, u32[]{:S(2)}) %collective-permute-start.5) | collective-permute-done | bytes 262176 | tf_op jit(solution)/shard_map/ppermute | solution.py:453
  22.7 0.7 copy-done.4
  23.4 1.4 %shard_map.95 = (bf16[128,1024]{1,0:T(8,128)(2,1)}, bf16[128,1280]{1,0:T(8,128)(2,1)S(1)}) custom-call(s32[32]{0:T(128)S(1)} %copy-done.4, bf16[128,1024]{1,0:T(8,128)(2,1)S(1)} %get-tuple-element.56.q0.b0, bf16[128,1024]{1,0:T(8,128)(2,1)S(1)} %collective-permute-done.3.q1.b1, bf16[128,1024]{1,0:T(8,128)(2,1)S(1)} %collective-permute-done.4.q2.b2, ...), custom_call_target="tpu_custom_call" | custom-call | bytes 1048576 | tf_op jit(solution)/shard_map/pallas_call | solution.py:102
  24.7 4.0 %collective-permute-start.9 = (bf16[128,1280]{1,0:T(8,128)(2,1)S(1)}, bf16[128,1280]{1,0:T(8,128)(2,1)S(1)}, u32[]{:S(2)}, u32[]{:S(2)}) collective-permute-start(bf16[128,1280]{1,0:T(8,128)(2,1)S(1)} %get-tuple-element.67), channel_id=1, source_target_pairs={{4,0},{6,2},{8,4},{10,6},{12,8},{14,10},{16,12},{18,14},{20,16},{2... | collective-permute-start | bytes 983048 | tf_op jit(solution)/shard_map/ppermute | solution.py:457
  28.7 3.3 %collective-permute-start.11 = (bf16[4,128,256]{2,1,0:T(8,128)(2,1)S(1)}, bf16[4,128,256]{2,1,0:T(8,128)(2,1)S(1)}, u32[]{:S(2)}, u32[]{:S(2)}) collective-permute-start(bf16[4,128,256]{2,1,0:T(8,128)(2,1)S(1)} %collective-permute-done.7.c2), channel_id=1, source_target_pairs={{0,8},{2,10},{4,12},{6,14},{8,16},{10,18},{12,20},{14,22},{16,24},... | collective-permute-start | bytes 786440 | tf_op jit(solution)/shard_map/ppermute | solution.py:457
  32.1 1.9 %collective-permute-start.8 = (bf16[128,1024]{1,0:T(8,128)(2,1)}, bf16[128,1024]{1,0:T(8,128)(2,1)S(1)}, u32[]{:S(2)}, u32[]{:S(2)}) collective-permute-start(bf16[128,1024]{1,0:T(8,128)(2,1)} %get-tuple-element.66), channel_id=1, source_target_pairs={{0,4},{2,6},{4,8},{6,10},{8,12},{10,14},{12,16},{14,18},{16,20},{1... | collective-permute-start | bytes 786440 | tf_op jit(solution)/shard_map/ppermute | solution.py:457
  34.0 0.6 shard_map.96
  34.6 0.7 collective-permute-start.12
  35.3 0.5 collective-permute-done.11.c4
  35.9 12.3 %collective-permute-done.8.b4 = bf16[128,1024]{1,0:T(8,128)(2,1)S(1)} collective-permute-done((bf16[128,1024]{1,0:T(8,128)(2,1)}, bf16[128,1024]{1,0:T(8,128)(2,1)S(1)}, u32[]{:S(2)}, u32[]{:S(2)}) %collective-permute-start.8) | collective-permute-done | bytes 262176 | tf_op jit(solution)/shard_map/ppermute | solution.py:457
  48.1 0.7 copy-done.5
  48.8 0.7 copy-done.6
  49.4 14.9 %shard_map.97 = (bf16[256,512]{1,0:T(8,128)(2,1)S(1)}, bf16[256,512]{1,0:T(8,128)(2,1)S(1)}, bf16[2,256,256]{2,1,0:T(8,128)(2,1)S(1)}, bf16[2,256,256]{2,1,0:T(8...) custom-call(s32[32]{0:T(128)S(1)} %copy-done.6, ...), custom_call_target="tpu_custom_call" | custom-call | flops 3221225472 | bytes 8388608 | tf_op jit(solution)/shard_map/pallas_call | solution.py:500
  64.4 1.9 %collective-permute-start.13 = (bf16[2,256,256]{2,1,0:T(8,128)(2,1)S(1)}, bf16[2,256,256]{2,1,0:T(8,128)(2,1)S(1)}, u32[]{:S(2)}, u32[]{:S(2)}) collective-permute-start(bf16[2,256,256]{2,1,0:T(8,128)(2,1)S(1)} %get-tuple-element.80), channel_id=1, source_target_pairs={{4,0},{6,2},{8,4},{10,6},{12,8},{14,10},{16,12},{18,14},{20,16},{2... | collective-permute-start | bytes 786440 | tf_op jit(solution)/shard_map/ppermute | solution.py:457
  66.3 1.9 %collective-permute-start.14 = (bf16[2,256,256]{2,1,0:T(8,128)(2,1)S(1)}, bf16[2,256,256]{2,1,0:T(8,128)(2,1)S(1)}, u32[]{:S(2)}, u32[]{:S(2)}) collective-permute-start(bf16[2,256,256]{2,1,0:T(8,128)(2,1)S(1)} %get-tuple-element.81), channel_id=1, source_target_pairs={{8,0},{10,2},{12,4},{14,6},{16,8},{18,10},{20,12},{22,14},{24,16},... | collective-permute-start | bytes 786440 | tf_op jit(solution)/shard_map/ppermute | solution.py:457
  68.2 10.0 %shard_map.98 = (bf16[256,512]{1,0:T(8,128)(2,1)S(1)}, bf16[256,512]{1,0:T(8,128)(2,1)S(1)}, bf16[2,256,256]{2,1,0:T(8,128)(2,1)S(1)}, bf16[2,256,256]{2,1,0:T(8,128)(2,1)S(1)}, bf16[2,256,256]{2,1,0:T(8,128)(2,1)S(1)}) custom-call(s32[32]{0:T(128)S(1)} %copy-done.6, bf16[2560,256]{1,0:T(8,128)(2,1)S(1)} %get-tuple-element.72.kv, ...), custom_call_target="tpu_custom_call" | custom-call | flops 3221225472 | bytes 8388608 | tf_op jit(solution)/shard_map/pallas_call | solution.py:520
  78.2 1.9 %collective-permute-start.19 = (bf16[2,256,256]{2,1,0:T(8,128)(2,1)S(1)}, bf16[2,256,256]{2,1,0:T(8,128)(2,1)S(1)}, u32[]{:S(2)}, u32[]{:S(2)}) collective-permute-start(bf16[2,256,256]{2,1,0:T(8,128)(2,1)S(1)} %get-tuple-element.89), channel_id=1, source_target_pairs={{4,0},{6,2},{8,4},{10,6},{12,8},{14,10},{16,12},{18,14},{20,16},{2... | collective-permute-start | bytes 786440 | tf_op jit(solution)/shard_map/ppermute | solution.py:457
  80.1 3.7 %collective-permute-start.18 = (bf16[256,512]{1,0:T(8,128)(2,1)S(1)}, bf16[256,512]{1,0:T(8,128)(2,1)S(1)}, u32[]{:S(2)}, u32[]{:S(2)}) collective-permute-start(bf16[256,512]{1,0:T(8,128)(2,1)S(1)} %get-tuple-element.85), channel_id=1, source_target_pairs={{0,2},{2,0},{4,6},{6,4},{8,10},{10,8},{12,14},{14,12},{16,18},{18,... | collective-permute-start | bytes 786440 | tf_op jit(solution)/shard_map/ppermute | solution.py:460
  83.8 0.1 collective-permute-start.17
  83.9 0.1 convert_add_fusion.1
  84.0 1.9 %collective-permute-start.15 = (bf16[256,256]{1,0:T(8,128)(2,1)S(1)}, bf16[256,256]{1,0:T(8,128)(2,1)S(1)}, u32[]{:S(2)}, u32[]{:S(2)}) collective-permute-start(bf16[256,256]{1,0:T(8,128)(2,1)S(1)} %get-tuple-element.93), channel_id=1, source_target_pairs={{8,0},{10,2},{12,4},{14,6},{16,8},{18,10},{20,12},{22,14},{24,16},... | collective-permute-start | bytes 393224 | tf_op jit(solution)/shard_map/ppermute | solution.py:457
  86.0 1.9 %collective-permute-start.16 = (bf16[256,256]{1,0:T(8,128)(2,1)S(1)}, bf16[256,256]{1,0:T(8,128)(2,1)S(1)}, u32[]{:S(2)}, u32[]{:S(2)}) collective-permute-start(bf16[256,256]{1,0:T(8,128)(2,1)S(1)} %get-tuple-element.92), channel_id=1, source_target_pairs={{8,2},{10,0},{12,6},{14,4},{16,10},{18,8},{20,14},{22,12},{24,18},... | collective-permute-start | bytes 393224 | tf_op jit(solution)/shard_map/ppermute | solution.py:554
  87.9 0.1 convert_add_fusion
  88.0 2.2 %collective-permute-start.20 = (bf16[256,256]{1,0:T(8,128)(2,1)S(1)}, bf16[256,256]{1,0:T(8,128)(2,1)S(1)}, u32[]{:S(2)}, u32[]{:S(2)}) collective-permute-start(bf16[256,256]{1,0:T(8,128)(2,1)S(1)} %fusion.4), channel_id=1, source_target_pairs={{0,2},{2,0},{4,6},{6,4},{8,10},{10,8},{12,14},{14,12},{16,18},{18,... | collective-permute-start | bytes 393224 | tf_op jit(solution)/shard_map/ppermute | solution.py:460
  90.2 0.9 maximum_select_fusion.1
  91.2 0.9 maximum_select_fusion
  92.1 1.8 %collective-permute-done.16 = bf16[256,256]{1,0:T(8,128)(2,1)S(1)} collective-permute-done((bf16[256,256]{1,0:T(8,128)(2,1)S(1)}, bf16[256,256]{1,0:T(8,128)(2,1)S(1)}, u32[]{:S(2)}, u32[]{:S(2)}) %collective-permute-start.16) | collective-permute-done | bytes 131104 | tf_op jit(solution)/shard_map/ppermute | solution.py:554
  94.0 0.1 fusion
  94.1 0.8 maximum_select_fusion.2
  (26 shorter events, 0.2 us)
Async XLA Ops:
  0.6 0.9 copy-start.2
  1.5 0.9 copy-start.3
  2.8 4.7 %collective-permute-start = (bf16[128,256]{1,0:T(8,128)(2,1)S(1)}, bf16[128,256]{1,0:T(8,128)(2,1)S(1)}, u32[]{:S(2)}, u32[]{:S(2)}) collective-permute-start(bf16[128,256]{1,0:T(8,128)(2,1)S(1)} %get-tuple-element.49), channel_id=1, source_target_pairs={{0,1},{1,0},{2,3},{3,2},{4,5},{5,4},{6,7},{7,6},{8,9},{9,8},{10,11... | collective-permute-start | bytes 196616 | tf_op jit(solution)/shard_map/ppermute | solution.py:453
  4.1 3.4 %collective-permute-start.1 = (bf16[128,256]{1,0:T(8,128)(2,1)S(1)}, bf16[128,256]{1,0:T(8,128)(2,1)S(1)}, u32[]{:S(2)}, u32[]{:S(2)}) collective-permute-start(bf16[128,256]{1,0:T(8,128)(2,1)S(1)} %get-tuple-element.50), channel_id=1, source_target_pairs={{0,2},{1,3},{2,0},{3,1},{4,6},{5,7},{6,4},{7,5},{8,10},{9,11},{10,... | collective-permute-start | bytes 196616 | tf_op jit(solution)/shard_map/ppermute | solution.py:453
  5.1 3.7 %collective-permute-start.2 = (bf16[128,256]{1,0:T(8,128)(2,1)S(1)}, bf16[128,256]{1,0:T(8,128)(2,1)S(1)}, u32[]{:S(2)}, u32[]{:S(2)}) collective-permute-start(bf16[128,256]{1,0:T(8,128)(2,1)S(1)} %get-tuple-element.51), channel_id=1, source_target_pairs={{0,3},{1,2},{2,1},{3,0},{4,7},{5,6},{6,5},{7,4},{8,11},{9,10},{10,... | collective-permute-start | bytes 196616 | tf_op jit(solution)/shard_map/ppermute | solution.py:453
  5.2 1.0 %copy-start = (bf16[128,2048]{1,0:T(8,128)(2,1)S(1)}, bf16[128,2048]{1,0:T(8,128)(2,1)}, u32[]{:S(2)}) copy-start(bf16[128,2048]{1,0:T(8,128)(2,1)} %one.3) | copy-start | bytes 1572868
  6.3 1.0 %copy-start.1 = (bf16[128,2048]{1,0:T(8,128)(2,1)S(1)}, bf16[128,2048]{1,0:T(8,128)(2,1)}, u32[]{:S(2)}) copy-start(bf16[128,2048]{1,0:T(8,128)(2,1)} %two.3) | copy-start | bytes 1572868
  8.8 8.3 %collective-permute-start.3 = (bf16[128,1024]{1,0:T(8,128)(2,1)S(1)}, bf16[128,1024]{1,0:T(8,128)(2,1)S(1)}, u32[]{:S(2)}, u32[]{:S(2)}) collective-permute-start(bf16[128,1024]{1,0:T(8,128)(2,1)S(1)} %get-tuple-element.57), channel_id=1, source_target_pairs={{0,1},{1,0},{2,3},{3,2},{4,5},{5,4},{6,7},{7,6},{8,9},{9,8},{10,11... | collective-permute-start | bytes 786440 | tf_op jit(solution)/shard_map/ppermute | solution.py:453
  9.7 11.1 %collective-permute-start.4 = (bf16[128,1024]{1,0:T(8,128)(2,1)S(1)}, bf16[128,1024]{1,0:T(8,128)(2,1)S(1)}, u32[]{:S(2)}, u32[]{:S(2)}) collective-permute-start(bf16[128,1024]{1,0:T(8,128)(2,1)S(1)} %get-tuple-element.58), channel_id=1, source_target_pairs={{0,2},{1,3},{2,0},{3,1},{4,6},{5,7},{6,4},{7,5},{8,10},{9,11},{10,... | collective-permute-start | bytes 786440 | tf_op jit(solution)/shard_map/ppermute | solution.py:453
  10.0 12.7 %collective-permute-start.5 = (bf16[128,1024]{1,0:T(8,128)(2,1)S(1)}, bf16[128,1024]{1,0:T(8,128)(2,1)S(1)}, u32[]{:S(2)}, u32[]{:S(2)}) collective-permute-start(bf16[128,1024]{1,0:T(8,128)(2,1)S(1)} %get-tuple-element.59), channel_id=1, source_target_pairs={{0,3},{1,2},{2,1},{3,0},{4,7},{5,6},{6,5},{7,4},{8,11},{9,10},{10,... | collective-permute-start | bytes 786440 | tf_op jit(solution)/shard_map/ppermute | solution.py:453
  10.7 14.1 %collective-permute-start.6 = (bf16[4,128,256]{2,1,0:T(8,128)(2,1)S(1)}, bf16[4,128,256]{2,1,0:T(8,128)(2,1)S(1)}, u32[]{:S(2)}, u32[]{:S(2)}) collective-permute-start(bf16[4,128,256]{2,1,0:T(8,128)(2,1)S(1)} %pad_maximum_fusion.c0), channel_id=1, source_target_pairs={{0,4},{2,6},{4,8},{6,10},{8,12},{10,14},{12,16},{14,18},{16,20},{1... | collective-permute-start | bytes 786440 | tf_op jit(solution)/shard_map/ppermute | solution.py:457
  13.8 10.9 %collective-permute-start.7 = (bf16[4,128,256]{2,1,0:T(8,128)(2,1)S(1)}, bf16[4,128,256]{2,1,0:T(8,128)(2,1)S(1)}, u32[]{:S(2)}, u32[]{:S(2)}) collective-permute-start(bf16[4,128,256]{2,1,0:T(8,128)(2,1)S(1)} %pad_maximum_fusion.c0), channel_id=1, source_target_pairs={{0,8},{2,10},{4,12},{6,14},{8,16},{10,18},{12,20},{14,22},{16,24},... | collective-permute-start | bytes 786440 | tf_op jit(solution)/shard_map/ppermute | solution.py:457
  17.1 17.6 %collective-permute-start.10 = (bf16[4,128,256]{2,1,0:T(8,128)(2,1)S(1)}, bf16[4,128,256]{2,1,0:T(8,128)(2,1)S(1)}, u32[]{:S(2)}, u32[]{:S(2)}) collective-permute-start(bf16[4,128,256]{2,1,0:T(8,128)(2,1)S(1)} %pad_maximum_fusion.c0), channel_id=1, source_target_pairs={{0,12},{2,14},{4,16},{6,18},{8,20},{10,22},{12,24},{14,26},{16,28}... | collective-permute-start | bytes 786440 | tf_op jit(solution)/shard_map/ppermute | solution.py:457
  22.7 0.7 copy-start.4
  24.7 23.4 %collective-permute-start.9 = (bf16[128,1280]{1,0:T(8,128)(2,1)S(1)}, bf16[128,1280]{1,0:T(8,128)(2,1)S(1)}, u32[]{:S(2)}, u32[]{:S(2)}) collective-permute-start(bf16[128,1280]{1,0:T(8,128)(2,1)S(1)} %get-tuple-element.67), channel_id=1, source_target_pairs={{4,0},{6,2},{8,4},{10,6},{12,8},{14,10},{16,12},{18,14},{20,16},{2... | collective-permute-start | bytes 983048 | tf_op jit(solution)/shard_map/ppermute | solution.py:457
  28.7 7.1 %collective-permute-start.11 = (bf16[4,128,256]{2,1,0:T(8,128)(2,1)S(1)}, bf16[4,128,256]{2,1,0:T(8,128)(2,1)S(1)}, u32[]{:S(2)}, u32[]{:S(2)}) collective-permute-start(bf16[4,128,256]{2,1,0:T(8,128)(2,1)S(1)} %collective-permute-done.7.c2), channel_id=1, source_target_pairs={{0,8},{2,10},{4,12},{6,14},{8,16},{10,18},{12,20},{14,22},{16,24},... | collective-permute-start | bytes 786440 | tf_op jit(solution)/shard_map/ppermute | solution.py:457
  32.1 16.1 %collective-permute-start.8 = (bf16[128,1024]{1,0:T(8,128)(2,1)}, bf16[128,1024]{1,0:T(8,128)(2,1)S(1)}, u32[]{:S(2)}, u32[]{:S(2)}) collective-permute-start(bf16[128,1024]{1,0:T(8,128)(2,1)} %get-tuple-element.66), channel_id=1, source_target_pairs={{0,4},{2,6},{4,8},{6,10},{8,12},{10,14},{12,16},{14,18},{16,20},{1... | collective-permute-start | bytes 786440 | tf_op jit(solution)/shard_map/ppermute | solution.py:457
  34.6 0.7 collective-permute-start.12
  48.1 0.7 copy-start.5
  48.8 0.7 copy-start.6
  64.4 19.5 %collective-permute-start.13 = (bf16[2,256,256]{2,1,0:T(8,128)(2,1)S(1)}, bf16[2,256,256]{2,1,0:T(8,128)(2,1)S(1)}, u32[]{:S(2)}, u32[]{:S(2)}) collective-permute-start(bf16[2,256,256]{2,1,0:T(8,128)(2,1)S(1)} %get-tuple-element.80), channel_id=1, source_target_pairs={{4,0},{6,2},{8,4},{10,6},{12,8},{14,10},{16,12},{18,14},{20,16},{2... | collective-permute-start | bytes 786440 | tf_op jit(solution)/shard_map/ppermute | solution.py:457
  66.3 17.6 %collective-permute-start.14 = (bf16[2,256,256]{2,1,0:T(8,128)(2,1)S(1)}, bf16[2,256,256]{2,1,0:T(8,128)(2,1)S(1)}, u32[]{:S(2)}, u32[]{:S(2)}) collective-permute-start(bf16[2,256,256]{2,1,0:T(8,128)(2,1)S(1)} %get-tuple-element.81), channel_id=1, source_target_pairs={{8,0},{10,2},{12,4},{14,6},{16,8},{18,10},{20,12},{22,14},{24,16},... | collective-permute-start | bytes 786440 | tf_op jit(solution)/shard_map/ppermute | solution.py:457
  78.2 9.7 %collective-permute-start.19 = (bf16[2,256,256]{2,1,0:T(8,128)(2,1)S(1)}, bf16[2,256,256]{2,1,0:T(8,128)(2,1)S(1)}, u32[]{:S(2)}, u32[]{:S(2)}) collective-permute-start(bf16[2,256,256]{2,1,0:T(8,128)(2,1)S(1)} %get-tuple-element.89), channel_id=1, source_target_pairs={{4,0},{6,2},{8,4},{10,6},{12,8},{14,10},{16,12},{18,14},{20,16},{2... | collective-permute-start | bytes 786440 | tf_op jit(solution)/shard_map/ppermute | solution.py:457
  80.1 10.1 %collective-permute-start.18 = (bf16[256,512]{1,0:T(8,128)(2,1)S(1)}, bf16[256,512]{1,0:T(8,128)(2,1)S(1)}, u32[]{:S(2)}, u32[]{:S(2)}) collective-permute-start(bf16[256,512]{1,0:T(8,128)(2,1)S(1)} %get-tuple-element.85), channel_id=1, source_target_pairs={{0,2},{2,0},{4,6},{6,4},{8,10},{10,8},{12,14},{14,12},{16,18},{18,... | collective-permute-start | bytes 786440 | tf_op jit(solution)/shard_map/ppermute | solution.py:460
  83.8 7.4 %collective-permute-start.17 = (bf16[256,512]{1,0:T(8,128)(2,1)S(1)}, bf16[256,512]{1,0:T(8,128)(2,1)S(1)}, u32[]{:S(2)}, u32[]{:S(2)}) collective-permute-start(bf16[256,512]{1,0:T(8,128)(2,1)S(1)} %get-tuple-element.83), channel_id=1, source_target_pairs={{0,2},{2,0},{4,6},{6,4},{8,10},{10,8},{12,14},{14,12},{16,18},{18,... | collective-permute-start | bytes 786440 | tf_op jit(solution)/shard_map/ppermute | solution.py:460
  84.0 8.1 %collective-permute-start.15 = (bf16[256,256]{1,0:T(8,128)(2,1)S(1)}, bf16[256,256]{1,0:T(8,128)(2,1)S(1)}, u32[]{:S(2)}, u32[]{:S(2)}) collective-permute-start(bf16[256,256]{1,0:T(8,128)(2,1)S(1)} %get-tuple-element.93), channel_id=1, source_target_pairs={{8,0},{10,2},{12,4},{14,6},{16,8},{18,10},{20,12},{22,14},{24,16},... | collective-permute-start | bytes 393224 | tf_op jit(solution)/shard_map/ppermute | solution.py:457
  86.0 8.0 %collective-permute-start.16 = (bf16[256,256]{1,0:T(8,128)(2,1)S(1)}, bf16[256,256]{1,0:T(8,128)(2,1)S(1)}, u32[]{:S(2)}, u32[]{:S(2)}) collective-permute-start(bf16[256,256]{1,0:T(8,128)(2,1)S(1)} %get-tuple-element.92), channel_id=1, source_target_pairs={{8,2},{10,0},{12,6},{14,4},{16,10},{18,8},{20,14},{22,12},{24,18},... | collective-permute-start | bytes 393224 | tf_op jit(solution)/shard_map/ppermute | solution.py:554
  88.0 6.0 %collective-permute-start.20 = (bf16[256,256]{1,0:T(8,128)(2,1)S(1)}, bf16[256,256]{1,0:T(8,128)(2,1)S(1)}, u32[]{:S(2)}, u32[]{:S(2)}) collective-permute-start(bf16[256,256]{1,0:T(8,128)(2,1)S(1)} %fusion.4), channel_id=1, source_target_pairs={{0,2},{2,0},{4,6},{6,4},{8,10},{10,8},{12,14},{14,12},{16,18},{18,... | collective-permute-start | bytes 393224 | tf_op jit(solution)/shard_map/ppermute | solution.py:460

commit v2 on v1

--- a/solution.py
+++ b/solution.py
@@ -81,11 +81,35 @@
     )(one, two)
 
 
-def move_kernel(home, q0, q1, q2, q3, k0, k1, k2, k3, right, left):
+def pack_joined_kernel(width, both, p0, p1, p2, p3):
+    unused, core_at, head_at = position()
+    total = both.shape[1] // 2
+    for target, (core_flip, head_flip) in zip((p0, p1, p2, p3), FLIPS):
+        group = SIDES * (head_at ^ head_flip) + (core_at ^ core_flip)
+        for which in range(2):
+            columns = pl.ds(pl.multiple_of(which * total + group * width, width), width)
+            target[:, which * width : (which + 1) * width] = both[:, columns]
+
+
+def pack_joined(both, groups):
+    rows, columns = both.shape
+    width = columns // (2 * groups)
+    packet = jax.ShapeDtypeStruct((rows, 2 * width), jnp.bfloat16)
+    return pl.pallas_call(
+        functools.partial(pack_joined_kernel, width),
+        out_shape=[packet] * 4,
+        in_specs=[VMEM],
+        out_specs=[VMEM] * 4,
+        compiler_params=SMALL,
+        cost_estimate=pl.CostEstimate(flops=0, bytes_accessed=4 * rows * columns, transcendentals=0),
+    )(both)
+
+
+def move_kernel(tables, q0, q1, q2, q3, k0, k1, k2, k3, right, left):
     chip_at, core_at, head_at = position()
     width = q0.shape[1]
     for slot, q, k in zip(local_slots(chip_at, core_at, head_at), (q0, q1, q2, q3), (k0, k1, k2, k3)):
-        target = home[slot] // (2 * SIDES)
+        target = tables[1, slot] // (2 * SIDES)
 
         @pl.when(target > chip_at)
         def _():
@@ -97,7 +121,7 @@
             left[:, width:] = k[...]
 
 
-def movers(home, queries, keys):
+def movers(tables, queries, keys):
     rows, width = queries[0].shape
     return pl.pallas_call(
         move_kernel,
@@ -109,18 +133,18 @@
         out_specs=[VMEM] * 2,
         compiler_params=SMALL,
         cost_estimate=pl.CostEstimate(flops=0, bytes_accessed=8 * rows * width, transcendentals=0),
-    )(home, *queries, *keys)
-
-
-def end_kernel(home, k0, k1, k2, k3, right):
+    )(tables, *queries, *keys)
+
+
+def end_kernel(tables, k0, k1, k2, k3, right):
     chip_at, core_at, head_at = position()
     for slot, ref in zip(local_slots(chip_at, core_at, head_at), (k0, k1, k2, k3)):
-        @pl.when(home[slot] // (2 * SIDES) > chip_at)
+        @pl.when(tables[1, slot] // (2 * SIDES) > chip_at)
         def _():
             right[...] = ref[...]
 
 
-def key_mover(home, keys):
+def key_mover(tables, keys):
     return pl.pallas_call(
         end_kernel,
         out_shape=jax.ShapeDtypeStruct(keys[0].shape, jnp.bfloat16),
@@ -130,7 +154,7 @@
         cost_estimate=pl.CostEstimate(
             flops=0, bytes_accessed=8 * keys[0].size, transcendentals=0
         ),
-    )(home, *keys)
+    )(tables, *keys)
 
 
 def block_sources(home, chip_at, core_at, head_at, b):
@@ -187,11 +211,11 @@
             g0 = e[:, :HEAD] * (dp[:, :HEAD] - delta)
             g1 = e[:, HEAD:] * (dp[:, HEAD:] - delta)
             ds = jnp.concatenate([g0, g1], axis=1).astype(jnp.bfloat16)
-            ds_low[i, rows] = ds
+            ds_low[i, 0, rows] = ds
             dq[i, rows] += dot(ds, kv[chunk(j), :HEAD], NN)
             if h % 2 == 1:
                 part = slice((h - 1) * tokens, (h + 1) * tokens)
-                term = dot(ds_low[i, part], q_stack[i, part], TN)
+                term = dot(ds_low[i, 0, part], q_stack[i, part], TN)
                 key_term = term if key_term is None else key_term + term
         return jnp.concatenate([key_term * ROOT, value_term], axis=1)
 
@@ -208,24 +232,72 @@
                 store(j, grad_terms(i, j).astype(jnp.bfloat16))
 
         return carry
+
+    def two_terms(i, j):
+        value_terms = [dot(e_low[i, j + step - i], do_stack[i], TN) for step in range(2)]
+        key_terms = [None, None]
+        for h in range(per_group):
+            rows = slice(h * tokens, (h + 1) * tokens)
+            delta = spread[i, rows]
+            parts = []
+            for step in range(2):
+                dp = dot(do_stack[i, rows], values_turned[j + step], NN)
+                e = e_low[i, j + step - i, rows].astype(jnp.float32)
+                g0 = e[:, :HEAD] * (dp[:, :HEAD] - delta)
+                g1 = e[:, HEAD:] * (dp[:, HEAD:] - delta)
+                ds = jnp.concatenate([g0, g1], axis=1).astype(jnp.bfloat16)
+                ds_low[i, step, rows] = ds
+                parts.append(ds)
+            keys = kv[pl.ds(pl.multiple_of(j * tokens, tokens), 2 * tokens), :HEAD]
+            dq[i, rows] += dot(jnp.concatenate(parts, axis=1), keys, NN)
+            if h % 2 == 1:
+                part = slice((h - 1) * tokens, (h + 1) * tokens)
+                for step in range(2):
+                    term = dot(ds_low[i, step, part], q_stack[i, part], TN)
+                    before = key_terms[step]
+                    key_terms[step] = term if before is None else before + term
+        return [
+            jnp.concatenate([key_terms[step] * ROOT, value_terms[step]], axis=1)
+            for step in range(2)
+        ]
 
     def no_terms(j, carry):
         store(j, jnp.zeros((tokens, 2 * HEAD), jnp.bfloat16))
         return carry
 
-    begin = jnp.clip(jnp.minimum(lowest[0], lowest[1]), start, stop)
-    lax.fori_loop(start, begin, no_terms, 0)
-    lax.fori_loop(begin, stop, grad_pass, 0)
+    def seen_by_both(j):
+        return (j >= lowest[0]) & (j >= lowest[1]) & (j < limit[0])
+
+    def two_pass(t, carry):
+        j = start + 2 * t
+        whole = seen_by_both(j) & seen_by_both(j + 1)
+
+        @pl.when(whole)
+        def _():
+            sums = [first + second for first, second in zip(two_terms(0, j), two_terms(1, j))]
+            for step in range(2):
+                store(j + step, sums[step].astype(jnp.bfloat16))
+
+        @pl.when(jnp.logical_not(whole))
+        def _():
+            begin = jnp.clip(jnp.minimum(lowest[0], lowest[1]), j, j + 2)
+            lax.fori_loop(j, begin, no_terms, 0)
+            lax.fori_loop(begin, j + 2, grad_pass, 0)
+
+        return carry
+
+    lax.fori_loop(0, (stop - start) // 2, two_pass, 0)
 
 
 def attention_kernel(
     per_group, tokens, shards,
-    docs, home, b0, b1, b2, b3, b4, b5, c0, c1, c2, c3, c4, end_far,
+    tables, b0, b1, b2, b3, b4, b5, c0, c1, c2, c3, c4, end_far,
     keep, send, d3, d4, kv, values_turned, e_low, spread, q_stack, do_stack, dq,
     ones, keys_turned, top, acc, ds_low, landed, end_near, sems,
 ):
     chip_at, core_at, head_at = position()
     q_width = per_group * HEAD
+    docs, home = tables.at[0], tables.at[1]
 
     def land(ref, b):
         return pltpu.make_async_copy(ref.at[:, pl.ds(0, 2 * q_width)], landed.at[b], sems.at[b])
@@ -351,6 +423,35 @@
             e_low[i, j - i, rows] = low
             acc[i, rows] += dot(low, ones[chunk(j)], NN)
 
+    def forward_two(i, j):
+        for h in range(per_group):
+            rows = head_rows(h)
+            m = top[i, rows]
+            lows = []
+            for step in range(2):
+                s = dot(q_stack[i, rows], keys_turned[j + step], NN)
+                e0 = jnp.exp2((s[:, :HEAD] - m) * EXP2_SCALE)
+                e1 = jnp.exp2((s[:, HEAD:] - m) * EXP2_SCALE)
+                low = jnp.concatenate([e0, e1], axis=1).astype(jnp.bfloat16)
+                e_low[i, j + step - i, rows] = low
+                lows.append(low)
+            values = ones[pl.ds(pl.multiple_of(j * tokens, tokens), 2 * tokens)]
+            acc[i, rows] += dot(jnp.concatenate(lows, axis=1), values, NN)
+
+    last_open = SIDES * BACK
+    open_count = jnp.int32(0)
+    for j in range(SIDES * BACK):
+        open_count = open_count + (is_open(0, j) & is_open(1, j)).astype(jnp.int32)
+    twos = open_count // 2
+
+    def two_pass(t, carry):
+        for i in range(SIDES):
+            forward_two(i, last_open - 2 * (t + 1))
+        return carry
+
+    def other_pass(t, carry):
+        return forward_pass(jnp.where(t < last_open - 2 * twos, t, t + 2 * twos), carry)
+
     def forward_pass(j, carry):
         open_all = is_open(0, j) & is_open(1, j)
 
@@ -371,7 +472,8 @@
         for i in range(SIDES):
             take_top(i, jnp.where(tries == 0, SIDES * BACK + i, lowest[i]))
         acc[...] = jnp.zeros_like(acc)
-        lax.fori_loop(begin, CHUNKS, forward_pass, 0)
+        lax.fori_loop(0, twos, two_pass, 0)
+        lax.fori_loop(begin, CHUNKS - 2 * twos, other_pass, 0)
         safe = jnp.min(jnp.where(acc[:, :, HEAD:] < SAFE_TOTAL, 1.0, 0.0))
         return tries + 1, (safe < 0.5).astype(jnp.int32)
 
@@ -411,11 +513,11 @@
 
 def second_kernel(
     per_group, tokens,
-    docs, kv, values_turned, e_low, spread, q_stack, do_stack, dq_first,
+    tables, kv, values_turned, e_low, spread, q_stack, do_stack, dq_first,
     keep, send, d0, d1, d2, dq, ds_low,
 ):
     chip_at, core_at, head_at = position()
-    unused, lowest, limit, begin = key_ranges(docs, chip_at)
+    unused, lowest, limit, begin = key_ranges(tables.at[0], chip_at)
     dq[...] = dq_first[...]
     gradient_loop(
         per_group, tokens, lowest, limit, SPLIT, CHUNKS, {0: d0, 1: d1, 2: d2},
@@ -467,7 +569,10 @@
             both(packets[3], 1, 1),
         ]
 
-    kv_packets = pack(key_states, value_vector_rows, groups)
+    tables = jnp.stack([doc_ids, block_home])
+    kv_packets = pack_joined(
+        jnp.concatenate([key_states, value_vector_rows], axis=1), groups
+    )
     qd_packets = pack(queries, grad_output, groups)
     kv_local, qd_packets = lax.optimization_barrier((exchange(kv_packets), qd_packets))
     own = jnp.stack(kv_local)
@@ -475,12 +580,12 @@
     two_back = along(own, 2 * SIDES)
     one_back = along(own, SIDES)
     three_back = along(own, 3 * SIDES)
-    kv_right = key_mover(block_home, kv_local)
-    right, left = movers(block_home, qd_local, kv_local)
-    right, left, one_back, two_back = lax.optimization_barrier((right, left, one_back, two_back))
+    kv_right = key_mover(tables, kv_local)
+    right, left = movers(tables, qd_local, kv_local)
+    right, left, two_back = lax.optimization_barrier((right, left, two_back))
     qd_all = qd_local + [along(right, SIDES), along(left, -SIDES)]
     four_back = along(two_back, 2 * SIDES)
-    three_back, kv_right = lax.optimization_barrier((three_back, kv_right))
+    one_back, three_back, kv_right = lax.optimization_barrier((one_back, three_back, kv_right))
     end_far = along(kv_right, SIDES * (BACK + 1))
 
     rows = per_group * tokens
@@ -500,14 +605,14 @@
     keep, send, d3, d4, *carried = pl.pallas_call(
         functools.partial(attention_kernel, per_group, tokens, shards),
         out_shape=[kept_shape] * 2 + [pair_shape] * 2 + state,
-        in_specs=[SMEM] * 2 + [ANY] * 6 + [VMEM] * 6,
+        in_specs=[SMEM] + [ANY] * 6 + [VMEM] * 6,
         out_specs=[VMEM] * (4 + len(state)),
         scratch_shapes=[
             pltpu.VMEM((CHUNKS * tokens, 2 * HEAD), jnp.bfloat16),
             pltpu.VMEM((CHUNKS, HEAD, tokens), jnp.bfloat16),
             pltpu.VMEM((SIDES, rows, HEAD), jnp.float32),
             pltpu.VMEM((SIDES, rows, 2 * HEAD), jnp.float32),
-            pltpu.VMEM((SIDES, rows, tokens), jnp.bfloat16),
+            pltpu.VMEM((SIDES, 2, rows, tokens), jnp.bfloat16),
             pltpu.VMEM((2 * SIDES, BLK, 2 * q_width), jnp.bfloat16),
             pltpu.VMEM((BLK, 2 * HEAD), jnp.bfloat16),
             pltpu.SemaphoreType.DMA((2 * SIDES + 1,)),
@@ -516,7 +621,7 @@
         cost_estimate=pl.CostEstimate(
             flops=work, bytes_accessed=8 * 1024 * 1024, transcendentals=work // (12 * HEAD)
         ),
-    )(doc_ids, block_home, *qd_all, own, one_back, two_back, three_back, four_back, end_far)
+    )(tables, *qd_all, own, one_back, two_back, three_back, four_back, end_far)
     dq_keep, dq_send, d0, d1, d2 = pl.pallas_call(
         functools.partial(second_kernel, per_group, tokens),
         out_shape=[kept_shape] * 2 + [pair_shape] * 3,
@@ -524,13 +629,13 @@
         out_specs=[VMEM] * 5,
         scratch_shapes=[
             pltpu.VMEM((SIDES, rows, HEAD), jnp.float32),
-            pltpu.VMEM((SIDES, rows, tokens), jnp.bfloat16),
+            pltpu.VMEM((SIDES, 2, rows, tokens), jnp.bfloat16),
         ],
         compiler_params=pltpu.CompilerParams(vmem_limit_bytes=8 * 1024 * 1024),
         cost_estimate=pl.CostEstimate(
             flops=work, bytes_accessed=8 * 1024 * 1024, transcendentals=0
         ),
-    )(doc_ids, *carried)
+    )(tables, *carried)
 
     def added(term, arrived):
         return term.astype(jnp.float32) + arrived.astype(jnp.float32)

time: 94.6 us -> 94.6 us (level); the launches traced: 94.9 us -> 93.4 us
  waiting for transfers between devices: 17.8 us -> 24.3 us
  starting transfers between devices: 39.8 us -> 34.8 us
  local copies, waits for them, and re-layouts: 5.87 us -> 2.11 us
  other arithmetic: 2.98 us -> 4.65 us
    ppermute x11, waiting for transfers between devices: 12.8 us -> 18.4 us  [along(): return lax.ppermute(array, 'seq', pairs)]
    unnamed x14 -> x4, local copies, waits for them, and re-layouts: 5.85 us -> 2.08 us
    ppermute x3, starting transfers between devices: 6.01 us -> 3.44 us  [core_swap(): return lax.ppermute(array, 'seq', [(s, s ^ 1) for s in everyone])]
    ppermute x11, starting transfers between devices: 27.7 us -> 25.2 us  [along(): return lax.ppermute(array, 'seq', pairs)]
    ppermute x6, waiting for transfers between devices: 3.16 us -> 4.17 us  [both(): return lax.ppermute(array, ('seq', 'head'), pairs)]
    concatenate x0 -> x1, other arithmetic: none -> 0.99 us  [per_device(): jnp.concatenate([key_states, value_vector_rows], axis=1)]
  transfers between devices with their start and end apart: 21 -> 21, of which waited for: 5 -> 6; matrix products, arithmetic and copies ran while one was open for 2% -> 3% of each run, Pallas kernels for 13% -> 13%
where the time goes in v2:
time: 94.6 us; the launch traced here: 93.4 us
  starting transfers between devices  34.8 us (37%)
  Pallas kernels  26.6 us (28%)
  waiting for transfers between devices  24.3 us (26%)
  other arithmetic  4.65 us (5%)
  local copies, waits for them, and re-layouts  2.11 us (2%)
    ppermute x11, starting transfers between devices, along(): return lax.ppermute(array, 'seq', pairs)  25.2 us
    ppermute x11, waiting for transfers between devices, along(): return lax.ppermute(array, 'seq', pairs)  18.4 us
    pallas_call x1, Pallas kernels, per_device(): pl.pallas_call(functools.partial(attention_kernel, per_group, tokens, sha...  14.8 us
    pallas_call x1, Pallas kernels, per_device(): pl.pallas_call(functools.partial(second_kernel, per_group, tokens), out_s...  9.53 us
    ppermute x6, starting transfers between devices, both(): return lax.ppermute(array, ('seq', 'head'), pairs)  4.24 us
    ppermute x6, waiting for transfers between devices, both(): return lax.ppermute(array, ('seq', 'head'), pairs)  4.17 us
    ppermute x3, starting transfers between devices, core_swap(): return lax.ppermute(array, 'seq', [(s, s ^ 1) for s in everyone])  3.44 us
    select_n x3, other arithmetic, joined(): jnp.where(first_core, jnp.concatenate([kept, taken], axis=1), jnp.concate...  2.66 us
  transfers between devices with their start and end apart: 21, of which 6 were waited for; matrix products, arithmetic and copies ran while one was open for 3% of the time, Pallas kernels for 13%

profile of v2, /device:TPU:17, one launch (start us, length us, event | category | flops | bytes accessed | tf_op | source)
XLA Modules:
  0.0 93.4 jit_solution(17246564551616827201)
XLA Ops:
  0.6 1.0 %pad_maximum_fusion.both = bf16[128,1024]{1,0:T(8,128)(2,1)S(1)} fusion(bf16[128,512]{1,0:T(8,128)(2,1)} %param.8, bf16[128,512]{1,0:T(8,128)(2,1)} %param.7), kind=kLoop, calls=%fused_computation.4 | loop fusion | flops 524288 | bytes 524288 | tf_op jit(solution)/shard_map/concatenate | solution.py:574
  1.6 0.1 shard_map.93
  1.7 1.3 %collective-permute-start = (bf16[128,256]{1,0:T(8,128)(2,1)S(1)}, bf16[128,256]{1,0:T(8,128)(2,1)S(1)}, u32[]{:S(2)}, u32[]{:S(2)}) collective-permute-start(bf16[128,256]{1,0:T(8,128)(2,1)S(1)} %get-tuple-element.49), channel_id=1, source_target_pairs={{0,1},{1,0},{2,3},{3,2},{4,5},{5,4},{6,7},{7,6},{8,9},{9,8},{10,11... | collective-permute-start | bytes 196616 | tf_op jit(solution)/shard_map/ppermute | solution.py:555
  3.0 1.0 %collective-permute-start.1 = (bf16[128,256]{1,0:T(8,128)(2,1)S(1)}, bf16[128,256]{1,0:T(8,128)(2,1)S(1)}, u32[]{:S(2)}, u32[]{:S(2)}) collective-permute-start(bf16[128,256]{1,0:T(8,128)(2,1)S(1)} %get-tuple-element.50), channel_id=1, source_target_pairs={{0,2},{1,3},{2,0},{3,1},{4,6},{5,7},{6,4},{7,5},{8,10},{9,11},{10,... | collective-permute-start | bytes 196616 | tf_op jit(solution)/shard_map/ppermute | solution.py:555
  4.0 0.1 collective-permute-start.2
  4.1 1.0 %copy-done = bf16[128,2048]{1,0:T(8,128)(2,1)S(1)} copy-done((bf16[128,2048]{1,0:T(8,128)(2,1)S(1)}, bf16[128,2048]{1,0:T(8,128)(2,1)}, u32[]{:S(2)}) %copy-start) | copy-done | bytes 524312
  5.1 1.0 %copy-done.1 = bf16[128,2048]{1,0:T(8,128)(2,1)S(1)} copy-done((bf16[128,2048]{1,0:T(8,128)(2,1)S(1)}, bf16[128,2048]{1,0:T(8,128)(2,1)}, u32[]{:S(2)}) %copy-start.1) | copy-done | bytes 524312
  6.2 0.2 shard_map.94
  6.4 0.0 collective-permute-done.k1
  6.4 1.3 %collective-permute-done.2.k3 = bf16[128,256]{1,0:T(8,128)(2,1)S(1)} collective-permute-done((bf16[128,256]{1,0:T(8,128)(2,1)S(1)}, bf16[128,256]{1,0:T(8,128)(2,1)S(1)}, u32[]{:S(2)}, u32[]{:S(2)}) %collective-permute-start.2) | collective-permute-done | bytes 65568 | tf_op jit(solution)/shard_map/ppermute | solution.py:555
  7.7 1.0 %collective-permute-start.3 = (bf16[128,1024]{1,0:T(8,128)(2,1)S(1)}, bf16[128,1024]{1,0:T(8,128)(2,1)S(1)}, u32[]{:S(2)}, u32[]{:S(2)}) collective-permute-start(bf16[128,1024]{1,0:T(8,128)(2,1)S(1)} %get-tuple-element.57), channel_id=1, source_target_pairs={{0,1},{1,0},{2,3},{3,2},{4,5},{5,4},{6,7},{7,6},{8,9},{9,8},{10,11... | collective-permute-start | bytes 786440 | tf_op jit(solution)/shard_map/ppermute | solution.py:555
  8.6 0.3 collective-permute-start.4
  8.9 0.6 collective-permute-start.5
  9.6 3.2 %collective-permute-start.6 = (bf16[4,128,256]{2,1,0:T(8,128)(2,1)S(1)}, bf16[4,128,256]{2,1,0:T(8,128)(2,1)S(1)}, u32[]{:S(2)}, u32[]{:S(2)}) collective-permute-start(bf16[4,128,256]{2,1,0:T(8,128)(2,1)S(1)} %pad_maximum_fusion.1.c0), channel_id=1, source_target_pairs={{0,8},{2,10},{4,12},{6,14},{8,16},{10,18},{12,20},{14,22},{16,24},... | collective-permute-start | bytes 786440 | tf_op jit(solution)/shard_map/ppermute | solution.py:559
  12.8 0.7 pad_add_fusion.tables
  13.5 2.2 %collective-permute-start.10 = (bf16[4,128,256]{2,1,0:T(8,128)(2,1)S(1)}, bf16[4,128,256]{2,1,0:T(8,128)(2,1)S(1)}, u32[]{:S(2)}, u32[]{:S(2)}) collective-permute-start(bf16[4,128,256]{2,1,0:T(8,128)(2,1)S(1)} %pad_maximum_fusion.1.c0), channel_id=1, source_target_pairs={{0,12},{2,14},{4,16},{6,18},{8,20},{10,22},{12,24},{14,26},{16,28}... | collective-permute-start | bytes 786440 | tf_op jit(solution)/shard_map/ppermute | solution.py:559
  15.7 0.0 collective-permute-done.3.q1.b1
  15.7 3.0 %collective-permute-start.9 = (bf16[4,128,256]{2,1,0:T(8,128)(2,1)S(1)}, bf16[4,128,256]{2,1,0:T(8,128)(2,1)S(1)}, u32[]{:S(2)}, u32[]{:S(2)}) collective-permute-start(bf16[4,128,256]{2,1,0:T(8,128)(2,1)S(1)} %pad_maximum_fusion.1.c0), channel_id=1, source_target_pairs={{0,4},{2,6},{4,8},{6,10},{8,12},{10,14},{12,16},{14,18},{16,20},{1... | collective-permute-start | bytes 786440 | tf_op jit(solution)/shard_map/ppermute | solution.py:559
  18.7 2.9 %collective-permute-done.5.q3.b3 = bf16[128,1024]{1,0:T(8,128)(2,1)S(1)} collective-permute-done((bf16[128,1024]{1,0:T(8,128)(2,1)S(1)}, bf16[128,1024]{1,0:T(8,128)(2,1)S(1)}, u32[]{:S(2)}, u32[]{:S(2)}) %collective-permute-start.5) | collective-permute-done | bytes 262176 | tf_op jit(solution)/shard_map/ppermute | solution.py:555
  21.6 1.4 %shard_map.95 = (bf16[128,1024]{1,0:T(8,128)(2,1)}, bf16[128,1280]{1,0:T(8,128)(2,1)S(1)}) custom-call(s32[2,32]{1,0:T(2,128)S(1)} %pad_add_fusion.tables, bf16[128,1024]{1,0:T(8,128)(2,1)S(1)} %get-tuple-element.56.q0.b0, bf16[128,1024]{1,0:T(8,128)(2,1)S(1)} %collective-permute-done.3.q1.b1, bf16[128,1024]{1,0:T(8,128)(2,1)S(1)} %collective-permute-done.4.q2.b2, ...), custom_call_target="tpu_custom_call" | custom-call | bytes 1048576 | tf_op jit(solution)/shard_map/pallas_call | solution.py:126
  23.0 3.0 %collective-permute-start.8 = (bf16[128,1280]{1,0:T(8,128)(2,1)S(1)}, bf16[128,1280]{1,0:T(8,128)(2,1)S(1)}, u32[]{:S(2)}, u32[]{:S(2)}) collective-permute-start(bf16[128,1280]{1,0:T(8,128)(2,1)S(1)} %get-tuple-element.67), channel_id=1, source_target_pairs={{4,0},{6,2},{8,4},{10,6},{12,8},{14,10},{16,12},{18,14},{20,16},{2... | collective-permute-start | bytes 983048 | tf_op jit(solution)/shard_map/ppermute | solution.py:559
  26.0 3.2 %collective-permute-start.11 = (bf16[4,128,256]{2,1,0:T(8,128)(2,1)S(1)}, bf16[4,128,256]{2,1,0:T(8,128)(2,1)S(1)}, u32[]{:S(2)}, u32[]{:S(2)}) collective-permute-start(bf16[4,128,256]{2,1,0:T(8,128)(2,1)S(1)} %collective-permute-done.6.c2), channel_id=1, source_target_pairs={{0,8},{2,10},{4,12},{6,14},{8,16},{10,18},{12,20},{14,22},{16,24},... | collective-permute-start | bytes 786440 | tf_op jit(solution)/shard_map/ppermute | solution.py:559
  29.2 2.0 %collective-permute-start.7 = (bf16[128,1024]{1,0:T(8,128)(2,1)}, bf16[128,1024]{1,0:T(8,128)(2,1)S(1)}, u32[]{:S(2)}, u32[]{:S(2)}) collective-permute-start(bf16[128,1024]{1,0:T(8,128)(2,1)} %get-tuple-element.66), channel_id=1, source_target_pairs={{0,4},{2,6},{4,8},{6,10},{8,12},{10,14},{12,16},{14,18},{16,20},{1... | collective-permute-start | bytes 786440 | tf_op jit(solution)/shard_map/ppermute | solution.py:559
  31.2 0.6 shard_map.96
  31.9 5.1 %collective-permute-done.9.c1 = bf16[4,128,256]{2,1,0:T(8,128)(2,1)S(1)} collective-permute-done((bf16[4,128,256]{2,1,0:T(8,128)(2,1)S(1)}, bf16[4,128,256]{2,1,0:T(8,128)(2,1)S(1)}, u32[]{:S(2)}, u32[]{:S(2)}) %collective-permute-start.9) | collective-permute-done | bytes 262176 | tf_op jit(solution)/shard_map/ppermute | solution.py:559
  37.0 0.7 collective-permute-start.12
  37.6 0.0 collective-permute-done.12.end_far
  37.7 11.9 %collective-permute-done.7.b4 = bf16[128,1024]{1,0:T(8,128)(2,1)S(1)} collective-permute-done((bf16[128,1024]{1,0:T(8,128)(2,1)}, bf16[128,1024]{1,0:T(8,128)(2,1)S(1)}, u32[]{:S(2)}, u32[]{:S(2)}) %collective-permute-start.7) | collective-permute-done | bytes 262176 | tf_op jit(solution)/shard_map/ppermute | solution.py:559
  49.6 0.0 collective-permute-done.8.b5
  49.6 14.8 %shard_map.97 = (bf16[256,512]{1,0:T(8,128)(2,1)S(1)}, bf16[256,512]{1,0:T(8,128)(2,1)S(1)}, bf16[2,256,256]{2,1,0:T(8,128)(2,1)S(1)}, bf16[2,256,256]{2,1,0:T(8...) custom-call(s32[2,32]{1,0:T(2,128)S(1)} %pad_add_fusion.tables, ...), custom_call_target="tpu_custom_call" | custom-call | flops 3221225472 | bytes 8388608 | tf_op jit(solution)/shard_map/pallas_call | solution.py:605
  64.4 1.9 %collective-permute-start.13 = (bf16[2,256,256]{2,1,0:T(8,128)(2,1)S(1)}, bf16[2,256,256]{2,1,0:T(8,128)(2,1)S(1)}, u32[]{:S(2)}, u32[]{:S(2)}) collective-permute-start(bf16[2,256,256]{2,1,0:T(8,128)(2,1)S(1)} %get-tuple-element.80), channel_id=1, source_target_pairs={{4,0},{6,2},{8,4},{10,6},{12,8},{14,10},{16,12},{18,14},{20,16},{2... | collective-permute-start | bytes 786440 | tf_op jit(solution)/shard_map/ppermute | solution.py:559
  66.4 2.1 %collective-permute-start.14 = (bf16[2,256,256]{2,1,0:T(8,128)(2,1)S(1)}, bf16[2,256,256]{2,1,0:T(8,128)(2,1)S(1)}, u32[]{:S(2)}, u32[]{:S(2)}) collective-permute-start(bf16[2,256,256]{2,1,0:T(8,128)(2,1)S(1)} %get-tuple-element.81), channel_id=1, source_target_pairs={{8,0},{10,2},{12,4},{14,6},{16,8},{18,10},{20,12},{22,14},{24,16},... | collective-permute-start | bytes 786440 | tf_op jit(solution)/shard_map/ppermute | solution.py:559
  68.5 9.5 %shard_map.98 = (bf16[256,512]{1,0:T(8,128)(2,1)S(1)}, bf16[256,512]{1,0:T(8,128)(2,1)S(1)}, bf16[2,256,256]{2,1,0:T(8,128)(2,1)S(1)}, bf16[2,256,256]{2,1,0:T(8,128)(2,1)S(1)}, bf16[2,256,256]{2,1,0:T(8,128)(2,1)S(1)}) custom-call(s32[2,32]{1,0:T(2,128)S(1)} %pad_add_fusion.tables, bf16[2560,256]{1,0:T(8,128)(2,1)S(1)} %get-tuple-element.72.kv, ...), custom_call_target="tpu_custom_call" | custom-call | flops 3221225472 | bytes 8388608 | tf_op jit(solution)/shard_map/pallas_call | solution.py:625
  78.0 1.9 %collective-permute-start.19 = (bf16[2,256,256]{2,1,0:T(8,128)(2,1)S(1)}, bf16[2,256,256]{2,1,0:T(8,128)(2,1)S(1)}, u32[]{:S(2)}, u32[]{:S(2)}) collective-permute-start(bf16[2,256,256]{2,1,0:T(8,128)(2,1)S(1)} %get-tuple-element.89), channel_id=1, source_target_pairs={{4,0},{6,2},{8,4},{10,6},{12,8},{14,10},{16,12},{18,14},{20,16},{2... | collective-permute-start | bytes 786440 | tf_op jit(solution)/shard_map/ppermute | solution.py:559
  80.0 1.2 %collective-permute-start.18 = (bf16[256,512]{1,0:T(8,128)(2,1)S(1)}, bf16[256,512]{1,0:T(8,128)(2,1)S(1)}, u32[]{:S(2)}, u32[]{:S(2)}) collective-permute-start(bf16[256,512]{1,0:T(8,128)(2,1)S(1)} %get-tuple-element.85), channel_id=1, source_target_pairs={{0,2},{2,0},{4,6},{6,4},{8,10},{10,8},{12,14},{14,12},{16,18},{18,... | collective-permute-start | bytes 786440 | tf_op jit(solution)/shard_map/ppermute | solution.py:562
  81.2 0.1 collective-permute-start.17
  81.3 0.0 collective-permute-done.13
  81.3 0.1 convert_add_fusion.1
  81.4 1.9 %collective-permute-start.15 = (bf16[256,256]{1,0:T(8,128)(2,1)S(1)}, bf16[256,256]{1,0:T(8,128)(2,1)S(1)}, u32[]{:S(2)}, u32[]{:S(2)}) collective-permute-start(bf16[256,256]{1,0:T(8,128)(2,1)S(1)} %get-tuple-element.93), channel_id=1, source_target_pairs={{8,0},{10,2},{12,4},{14,6},{16,8},{18,10},{20,12},{22,14},{24,16},... | collective-permute-start | bytes 393224 | tf_op jit(solution)/shard_map/ppermute | solution.py:559
  83.3 1.9 %collective-permute-start.16 = (bf16[256,256]{1,0:T(8,128)(2,1)S(1)}, bf16[256,256]{1,0:T(8,128)(2,1)S(1)}, u32[]{:S(2)}, u32[]{:S(2)}) collective-permute-start(bf16[256,256]{1,0:T(8,128)(2,1)S(1)} %get-tuple-element.92), channel_id=1, source_target_pairs={{8,2},{10,0},{12,6},{14,4},{16,10},{18,8},{20,14},{22,12},{24,18},... | collective-permute-start | bytes 393224 | tf_op jit(solution)/shard_map/ppermute | solution.py:659
  85.3 1.3 %collective-permute-done.19 = bf16[2,256,256]{2,1,0:T(8,128)(2,1)S(1)} collective-permute-done((bf16[2,256,256]{2,1,0:T(8,128)(2,1)S(1)}, bf16[2,256,256]{2,1,0:T(8,128)(2,1)S(1)}, u32[]{:S(2)}, u32[]{:S(2)}) %collective-permute-start.19) | collective-permute-done | bytes 262176 | tf_op jit(solution)/shard_map/ppermute | solution.py:559
  86.6 0.1 convert_add_fusion
  86.7 2.1 %collective-permute-start.20 = (bf16[256,256]{1,0:T(8,128)(2,1)S(1)}, bf16[256,256]{1,0:T(8,128)(2,1)S(1)}, u32[]{:S(2)}, u32[]{:S(2)}) collective-permute-start(bf16[256,256]{1,0:T(8,128)(2,1)S(1)} %fusion.4), channel_id=1, source_target_pairs={{0,2},{2,0},{4,6},{6,4},{8,10},{10,8},{12,14},{14,12},{16,18},{18,... | collective-permute-start | bytes 393224 | tf_op jit(solution)/shard_map/ppermute | solution.py:562
  88.8 0.9 %maximum_select_fusion.1 = bf16[256,1024]{1,0:T(8,128)(2,1)} fusion(bf16[256,512]{1,0:T(8,128)(2,1)S(1)} %collective-permute-done.18, bf16[256,512]{1,0:T(8,128)(2,1)S(1)} %get-tuple-element.84, pred[]{:T(512)S(6)} %eq.5), kind=kLoop, calls=%fused_computation.1 | loop fusion | flops 2359296 | bytes 1048577 | tf_op jit(solution)/shard_map/jit(_where)/select_n | solution.py:663
  89.8 0.9 %maximum_select_fusion = bf16[256,1024]{1,0:T(8,128)(2,1)} fusion(bf16[256,512]{1,0:T(8,128)(2,1)S(1)} %collective-permute-done.17, bf16[256,512]{1,0:T(8,128)(2,1)S(1)} %get-tuple-element.82, pred[]{:T(512)S(6)} %eq.5), kind=kLoop, calls=%fused_computation | loop fusion | flops 2359296 | bytes 1048577 | tf_op jit(solution)/shard_map/jit(_where)/select_n | solution.py:663
  90.7 1.8 %collective-permute-done.16 = bf16[256,256]{1,0:T(8,128)(2,1)S(1)} collective-permute-done((bf16[256,256]{1,0:T(8,128)(2,1)S(1)}, bf16[256,256]{1,0:T(8,128)(2,1)S(1)}, u32[]{:S(2)}, u32[]{:S(2)}) %collective-permute-start.16) | collective-permute-done | bytes 131104 | tf_op jit(solution)/shard_map/ppermute | solution.py:659
  92.5 0.1 fusion
  92.6 0.8 maximum_select_fusion.2
  (18 shorter events, 0.2 us)
Async XLA Ops:
  1.7 4.7 %collective-permute-start = (bf16[128,256]{1,0:T(8,128)(2,1)S(1)}, bf16[128,256]{1,0:T(8,128)(2,1)S(1)}, u32[]{:S(2)}, u32[]{:S(2)}) collective-permute-start(bf16[128,256]{1,0:T(8,128)(2,1)S(1)} %get-tuple-element.49), channel_id=1, source_target_pairs={{0,1},{1,0},{2,3},{3,2},{4,5},{5,4},{6,7},{7,6},{8,9},{9,8},{10,11... | collective-permute-start | bytes 196616 | tf_op jit(solution)/shard_map/ppermute | solution.py:555
  3.0 3.4 %collective-permute-start.1 = (bf16[128,256]{1,0:T(8,128)(2,1)S(1)}, bf16[128,256]{1,0:T(8,128)(2,1)S(1)}, u32[]{:S(2)}, u32[]{:S(2)}) collective-permute-start(bf16[128,256]{1,0:T(8,128)(2,1)S(1)} %get-tuple-element.50), channel_id=1, source_target_pairs={{0,2},{1,3},{2,0},{3,1},{4,6},{5,7},{6,4},{7,5},{8,10},{9,11},{10,... | collective-permute-start | bytes 196616 | tf_op jit(solution)/shard_map/ppermute | solution.py:555
  4.0 3.7 %collective-permute-start.2 = (bf16[128,256]{1,0:T(8,128)(2,1)S(1)}, bf16[128,256]{1,0:T(8,128)(2,1)S(1)}, u32[]{:S(2)}, u32[]{:S(2)}) collective-permute-start(bf16[128,256]{1,0:T(8,128)(2,1)S(1)} %get-tuple-element.51), channel_id=1, source_target_pairs={{0,3},{1,2},{2,1},{3,0},{4,7},{5,6},{6,5},{7,4},{8,11},{9,10},{10,... | collective-permute-start | bytes 196616 | tf_op jit(solution)/shard_map/ppermute | solution.py:555
  4.1 1.0 %copy-start = (bf16[128,2048]{1,0:T(8,128)(2,1)S(1)}, bf16[128,2048]{1,0:T(8,128)(2,1)}, u32[]{:S(2)}) copy-start(bf16[128,2048]{1,0:T(8,128)(2,1)} %one.1) | copy-start | bytes 1572868
  5.1 1.0 %copy-start.1 = (bf16[128,2048]{1,0:T(8,128)(2,1)S(1)}, bf16[128,2048]{1,0:T(8,128)(2,1)}, u32[]{:S(2)}) copy-start(bf16[128,2048]{1,0:T(8,128)(2,1)} %two.1) | copy-start | bytes 1572868
  7.7 8.0 %collective-permute-start.3 = (bf16[128,1024]{1,0:T(8,128)(2,1)S(1)}, bf16[128,1024]{1,0:T(8,128)(2,1)S(1)}, u32[]{:S(2)}, u32[]{:S(2)}) collective-permute-start(bf16[128,1024]{1,0:T(8,128)(2,1)S(1)} %get-tuple-element.57), channel_id=1, source_target_pairs={{0,1},{1,0},{2,3},{3,2},{4,5},{5,4},{6,7},{7,6},{8,9},{9,8},{10,11... | collective-permute-start | bytes 786440 | tf_op jit(solution)/shard_map/ppermute | solution.py:555
  8.6 10.1 %collective-permute-start.4 = (bf16[128,1024]{1,0:T(8,128)(2,1)S(1)}, bf16[128,1024]{1,0:T(8,128)(2,1)S(1)}, u32[]{:S(2)}, u32[]{:S(2)}) collective-permute-start(bf16[128,1024]{1,0:T(8,128)(2,1)S(1)} %get-tuple-element.58), channel_id=1, source_target_pairs={{0,2},{1,3},{2,0},{3,1},{4,6},{5,7},{6,4},{7,5},{8,10},{9,11},{10,... | collective-permute-start | bytes 786440 | tf_op jit(solution)/shard_map/ppermute | solution.py:555
  8.9 12.7 %collective-permute-start.5 = (bf16[128,1024]{1,0:T(8,128)(2,1)S(1)}, bf16[128,1024]{1,0:T(8,128)(2,1)S(1)}, u32[]{:S(2)}, u32[]{:S(2)}) collective-permute-start(bf16[128,1024]{1,0:T(8,128)(2,1)S(1)} %get-tuple-element.59), channel_id=1, source_target_pairs={{0,3},{1,2},{2,1},{3,0},{4,7},{5,6},{6,5},{7,4},{8,11},{9,10},{10,... | collective-permute-start | bytes 786440 | tf_op jit(solution)/shard_map/ppermute | solution.py:555
  9.6 13.4 %collective-permute-start.6 = (bf16[4,128,256]{2,1,0:T(8,128)(2,1)S(1)}, bf16[4,128,256]{2,1,0:T(8,128)(2,1)S(1)}, u32[]{:S(2)}, u32[]{:S(2)}) collective-permute-start(bf16[4,128,256]{2,1,0:T(8,128)(2,1)S(1)} %pad_maximum_fusion.1.c0), channel_id=1, source_target_pairs={{0,8},{2,10},{4,12},{6,14},{8,16},{10,18},{12,20},{14,22},{16,24},... | collective-permute-start | bytes 786440 | tf_op jit(solution)/shard_map/ppermute | solution.py:559
  13.5 18.4 %collective-permute-start.10 = (bf16[4,128,256]{2,1,0:T(8,128)(2,1)S(1)}, bf16[4,128,256]{2,1,0:T(8,128)(2,1)S(1)}, u32[]{:S(2)}, u32[]{:S(2)}) collective-permute-start(bf16[4,128,256]{2,1,0:T(8,128)(2,1)S(1)} %pad_maximum_fusion.1.c0), channel_id=1, source_target_pairs={{0,12},{2,14},{4,16},{6,18},{8,20},{10,22},{12,24},{14,26},{16,28}... | collective-permute-start | bytes 786440 | tf_op jit(solution)/shard_map/ppermute | solution.py:559
  15.7 21.3 %collective-permute-start.9 = (bf16[4,128,256]{2,1,0:T(8,128)(2,1)S(1)}, bf16[4,128,256]{2,1,0:T(8,128)(2,1)S(1)}, u32[]{:S(2)}, u32[]{:S(2)}) collective-permute-start(bf16[4,128,256]{2,1,0:T(8,128)(2,1)S(1)} %pad_maximum_fusion.1.c0), channel_id=1, source_target_pairs={{0,4},{2,6},{4,8},{6,10},{8,12},{10,14},{12,16},{14,18},{16,20},{1... | collective-permute-start | bytes 786440 | tf_op jit(solution)/shard_map/ppermute | solution.py:559
  23.0 26.6 %collective-permute-start.8 = (bf16[128,1280]{1,0:T(8,128)(2,1)S(1)}, bf16[128,1280]{1,0:T(8,128)(2,1)S(1)}, u32[]{:S(2)}, u32[]{:S(2)}) collective-permute-start(bf16[128,1280]{1,0:T(8,128)(2,1)S(1)} %get-tuple-element.67), channel_id=1, source_target_pairs={{4,0},{6,2},{8,4},{10,6},{12,8},{14,10},{16,12},{18,14},{20,16},{2... | collective-permute-start | bytes 983048 | tf_op jit(solution)/shard_map/ppermute | solution.py:559
  26.0 11.6 %collective-permute-start.11 = (bf16[4,128,256]{2,1,0:T(8,128)(2,1)S(1)}, bf16[4,128,256]{2,1,0:T(8,128)(2,1)S(1)}, u32[]{:S(2)}, u32[]{:S(2)}) collective-permute-start(bf16[4,128,256]{2,1,0:T(8,128)(2,1)S(1)} %collective-permute-done.6.c2), channel_id=1, source_target_pairs={{0,8},{2,10},{4,12},{6,14},{8,16},{10,18},{12,20},{14,22},{16,24},... | collective-permute-start | bytes 786440 | tf_op jit(solution)/shard_map/ppermute | solution.py:559
  29.2 20.4 %collective-permute-start.7 = (bf16[128,1024]{1,0:T(8,128)(2,1)}, bf16[128,1024]{1,0:T(8,128)(2,1)S(1)}, u32[]{:S(2)}, u32[]{:S(2)}) collective-permute-start(bf16[128,1024]{1,0:T(8,128)(2,1)} %get-tuple-element.66), channel_id=1, source_target_pairs={{0,4},{2,6},{4,8},{6,10},{8,12},{10,14},{12,16},{14,18},{16,20},{1... | collective-permute-start | bytes 786440 | tf_op jit(solution)/shard_map/ppermute | solution.py:559
  37.0 0.7 collective-permute-start.12
  64.4 16.8 %collective-permute-start.13 = (bf16[2,256,256]{2,1,0:T(8,128)(2,1)S(1)}, bf16[2,256,256]{2,1,0:T(8,128)(2,1)S(1)}, u32[]{:S(2)}, u32[]{:S(2)}) collective-permute-start(bf16[2,256,256]{2,1,0:T(8,128)(2,1)S(1)} %get-tuple-element.80), channel_id=1, source_target_pairs={{4,0},{6,2},{8,4},{10,6},{12,8},{14,10},{16,12},{18,14},{20,16},{2... | collective-permute-start | bytes 786440 | tf_op jit(solution)/shard_map/ppermute | solution.py:559
  66.4 14.9 %collective-permute-start.14 = (bf16[2,256,256]{2,1,0:T(8,128)(2,1)S(1)}, bf16[2,256,256]{2,1,0:T(8,128)(2,1)S(1)}, u32[]{:S(2)}, u32[]{:S(2)}) collective-permute-start(bf16[2,256,256]{2,1,0:T(8,128)(2,1)S(1)} %get-tuple-element.81), channel_id=1, source_target_pairs={{8,0},{10,2},{12,4},{14,6},{16,8},{18,10},{20,12},{22,14},{24,16},... | collective-permute-start | bytes 786440 | tf_op jit(solution)/shard_map/ppermute | solution.py:559
  78.0 8.5 %collective-permute-start.19 = (bf16[2,256,256]{2,1,0:T(8,128)(2,1)S(1)}, bf16[2,256,256]{2,1,0:T(8,128)(2,1)S(1)}, u32[]{:S(2)}, u32[]{:S(2)}) collective-permute-start(bf16[2,256,256]{2,1,0:T(8,128)(2,1)S(1)} %get-tuple-element.89), channel_id=1, source_target_pairs={{4,0},{6,2},{8,4},{10,6},{12,8},{14,10},{16,12},{18,14},{20,16},{2... | collective-permute-start | bytes 786440 | tf_op jit(solution)/shard_map/ppermute | solution.py:559
  80.0 8.9 %collective-permute-start.18 = (bf16[256,512]{1,0:T(8,128)(2,1)S(1)}, bf16[256,512]{1,0:T(8,128)(2,1)S(1)}, u32[]{:S(2)}, u32[]{:S(2)}) collective-permute-start(bf16[256,512]{1,0:T(8,128)(2,1)S(1)} %get-tuple-element.85), channel_id=1, source_target_pairs={{0,2},{2,0},{4,6},{6,4},{8,10},{10,8},{12,14},{14,12},{16,18},{18,... | collective-permute-start | bytes 786440 | tf_op jit(solution)/shard_map/ppermute | solution.py:562
  81.2 8.6 %collective-permute-start.17 = (bf16[256,512]{1,0:T(8,128)(2,1)S(1)}, bf16[256,512]{1,0:T(8,128)(2,1)S(1)}, u32[]{:S(2)}, u32[]{:S(2)}) collective-permute-start(bf16[256,512]{1,0:T(8,128)(2,1)S(1)} %get-tuple-element.83), channel_id=1, source_target_pairs={{0,2},{2,0},{4,6},{6,4},{8,10},{10,8},{12,14},{14,12},{16,18},{18,... | collective-permute-start | bytes 786440 | tf_op jit(solution)/shard_map/ppermute | solution.py:562
  81.4 9.3 %collective-permute-start.15 = (bf16[256,256]{1,0:T(8,128)(2,1)S(1)}, bf16[256,256]{1,0:T(8,128)(2,1)S(1)}, u32[]{:S(2)}, u32[]{:S(2)}) collective-permute-start(bf16[256,256]{1,0:T(8,128)(2,1)S(1)} %get-tuple-element.93), channel_id=1, source_target_pairs={{8,0},{10,2},{12,4},{14,6},{16,8},{18,10},{20,12},{22,14},{24,16},... | collective-permute-start | bytes 393224 | tf_op jit(solution)/shard_map/ppermute | solution.py:559
  83.3 9.1 %collective-permute-start.16 = (bf16[256,256]{1,0:T(8,128)(2,1)S(1)}, bf16[256,256]{1,0:T(8,128)(2,1)S(1)}, u32[]{:S(2)}, u32[]{:S(2)}) collective-permute-start(bf16[256,256]{1,0:T(8,128)(2,1)S(1)} %get-tuple-element.92), channel_id=1, source_target_pairs={{8,2},{10,0},{12,6},{14,4},{16,10},{18,8},{20,14},{22,12},{24,18},... | collective-permute-start | bytes 393224 | tf_op jit(solution)/shard_map/ppermute | solution.py:659
  86.7 5.9 %collective-permute-start.20 = (bf16[256,256]{1,0:T(8,128)(2,1)S(1)}, bf16[256,256]{1,0:T(8,128)(2,1)S(1)}, u32[]{:S(2)}, u32[]{:S(2)}) collective-permute-start(bf16[256,256]{1,0:T(8,128)(2,1)S(1)} %fusion.4), channel_id=1, source_target_pairs={{0,2},{2,0},{4,6},{6,4},{8,10},{10,8},{12,14},{14,12},{16,18},{18,... | collective-permute-start | bytes 393224 | tf_op jit(solution)/shard_map/ppermute | solution.py:562
